TPU v7x, 32 devices: a whole 2x2x4 slice. The times are simulated.
32 devices in a mesh: pb: 8 (over y, x, core), pa: 4 (over z).
Axes of the slice: x: 2, y: 2, z: 4, core: 2. Of those that a mesh axis runs over, the one named last changes fastest.
Arguments:
- query_kv: bfloat16 [32, 2, 32, 1024], P(('pb', 'pa')), may hold values from -20 to 20
- student_query: bfloat16 [32, 1024], P(('pb', 'pa')), may hold values from -6 to 6
- block_holder: int32 [32, 2, 1], P('pb'), may hold values from 0 to 3; in each aligned block of 8 rows (0 to 7, 8 to 15, ..., all dimensions but the last counted through in order) at most 4 rows name the same one
- cand_local: int32 [32, 2, 32], P('pb'), may hold values from 0 to 63, all different within a row
- counts: int32 [32], P('pb'), may hold values from 1 to 64
- passage_qkv: bfloat16 [256, 3, 32, 1024], P(('pa', 'pb')), may hold values from -20 to 20
- passage_resid: bfloat16 [256, 1024], P(('pa', 'pb')), may hold values from -6 to 6
- student_passage: bfloat16 [256, 1024], P(('pa', 'pb')), may hold values from -6 to 6
- w_o: bfloat16 [1024, 1024], replicated, may hold values from -0.1875 to 0.1875
- ln_gain: float32 [1024], replicated, may hold values from 0.5 to 1.5
- ln_bias: float32 [1024], replicated, may hold values from -3 to 3
- w_dense: bfloat16 [1024, 1024], replicated, may hold values from -0.1875 to 0.1875
- b_dense: float32 [1024], replicated, may hold values from -3 to 3
- w_out: float32 [1024], replicated, may hold values from -0.6 to 0.6
Outputs:
- teacher_scores: float32 [32, 64], P(('pb', 'pa'))
- query_loss: float32 [32], P(('pb', 'pa'))
- grad_query: float32 [32, 1024], P(('pb', 'pa'))
- grad_passage: float32 [256, 1024], P(('pa', 'pb'))
Inputs may be any that keep to these rules, and one draw needn't show every extreme that they name: `block_holder`: among the 8 candidate blocks of the queries of one index of pb, padding blocks included, no holder is named more than 4 times; in some index of pb one holder is named exactly 4 times. `cand_local`: the 32 entries of one block are distinct. Slots from counts[q] on are padding.
All inputs are finite; a program needn't handle non-finite values.
Results may differ from a plain program's by a relative error of at most 0.0038.
Values may be sent and summed in bfloat16 or wider, within the bound.
A program may use at most 128 MiB of HBM per device.

v0:
```python
import jax
import jax.numpy as jnp
from jax import lax
from jax.sharding import PartitionSpec as P

HEADS = 16
HOLD_CAP = 4


student_scale = 0.125
norm_eps = 1e-05


def self_attend(block_qkv):
    passage_count, _, length, feature_width = block_qkv.shape
    head_dim = feature_width // HEADS
    split_qkv = block_qkv.reshape(passage_count, 3, length, HEADS, head_dim)
    scores = jnp.einsum(
        "pthd,puhd->phtu", split_qkv[:, 0], split_qkv[:, 1], preferred_element_type=jnp.float32
    ) * head_dim ** (-0.5)
    row_max = jnp.max(scores, axis=-1, keepdims=True)
    scaled = jnp.exp(scores - row_max)
    row_total = jnp.sum(scaled, axis=-1, keepdims=True)
    self_lse = (row_max + jnp.log(row_total))[..., 0]
    self_probs = (scaled / row_total).astype(jnp.bfloat16)
    self_out = jnp.einsum(
        "phtu,puhd->pthd", self_probs, split_qkv[:, 2], preferred_element_type=jnp.float32
    )
    return (self_out.reshape(passage_count, length, feature_width).astype(jnp.bfloat16), self_lse)


def score_block(pass_q, pass_o, pass_lse, pass_resid, key_val, weights):
    w_o, ln_gain, ln_bias, w_dense, b_dense, w_out = weights
    passage_count, length, feature_width = pass_q.shape
    head_dim = feature_width // HEADS
    query_len = key_val.shape[1]
    token_rows = pass_q.reshape(passage_count * length, HEADS, head_dim)
    key_rows = key_val[0].reshape(query_len, HEADS, head_dim)
    value_rows = key_val[1].reshape(query_len, HEADS, head_dim)
    scores = jnp.einsum(
        "rhd,ahd->har", token_rows, key_rows, preferred_element_type=jnp.float32
    ) * head_dim ** (-0.5)
    row_max = jnp.max(scores, axis=1, keepdims=True)
    scaled = jnp.exp(scores - row_max)
    row_total = jnp.sum(scaled, axis=1, keepdims=True)
    cross_lse = row_max[:, 0, :] + jnp.log(row_total[:, 0, :])
    self_lse = jnp.transpose(pass_lse, (1, 0, 2)).reshape(HEADS, passage_count * length)
    self_share = jax.nn.sigmoid(self_lse - cross_lse)
    spread = (1.0 - self_share)[:, None, :] * scaled / row_total
    key_weight = (
        jnp.sum(spread.reshape(HEADS, query_len, passage_count, length), axis=3) / length
    ).astype(jnp.bfloat16)
    query_part = jnp.einsum(
        "hab,ahd->bhd", key_weight, value_rows, preferred_element_type=jnp.float32
    ).reshape(passage_count, feature_width)
    token_weight = (self_share / length).astype(jnp.bfloat16).reshape(HEADS, passage_count, length)
    self_rows = pass_o.reshape(passage_count, length, HEADS, head_dim)
    self_part = jnp.einsum(
        "hbt,bthd->bhd", token_weight, self_rows, preferred_element_type=jnp.float32
    ).reshape(passage_count, feature_width)
    pooled = (query_part + self_part).astype(jnp.bfloat16)
    mixed_rows = jnp.dot(pooled, w_o, preferred_element_type=jnp.float32) + pass_resid.astype(
        jnp.float32
    )
    row_mean = jnp.mean(mixed_rows, axis=-1, keepdims=True)
    centered = mixed_rows - row_mean
    row_var = jnp.mean(centered * centered, axis=-1, keepdims=True)
    normed = (centered * lax.rsqrt(row_var + norm_eps) * ln_gain + ln_bias).astype(jnp.bfloat16)
    hidden = jnp.tanh(jnp.dot(normed, w_dense, preferred_element_type=jnp.float32) + b_dense)
    return jnp.sum(hidden * w_out, axis=-1)


def log_probs(scores, is_valid):
    masked = jnp.where(is_valid, scores, jnp.float32(-1e30))
    row_max = jnp.max(masked, axis=-1, keepdims=True)
    scaled = jnp.where(is_valid, jnp.exp(masked - row_max), jnp.float32(0.0))
    return scores - row_max - jnp.log(jnp.sum(scaled, axis=-1, keepdims=True))


def distill(teacher, student, is_valid):
    log_t = log_probs(teacher, is_valid)
    log_s = log_probs(student, is_valid)
    prob_t = jnp.where(is_valid, jnp.exp(log_t), jnp.float32(0.0))
    prob_s = jnp.where(is_valid, jnp.exp(log_s), jnp.float32(0.0))
    loss = jnp.sum(jnp.where(is_valid, prob_t * (log_t - log_s), jnp.float32(0.0)), axis=-1)
    return (loss, prob_s - prob_t)


def local(
    query_kv,
    student_query,
    block_holder,
    cand_local,
    counts,
    passage_qkv,
    passage_resid,
    student_passage,
    w_o,
    ln_gain,
    ln_bias,
    w_dense,
    b_dense,
    w_out,
):
    weights = (w_o, ln_gain, ln_bias, w_dense, b_dense, w_out)
    highest = lax.Precision.HIGHEST
    q_dev = query_kv.shape[0]
    blocks = block_holder.shape[1]
    slot_len = cand_local.shape[2]
    group_rows = block_holder.shape[0]
    column_index = lax.axis_index("pa")
    row_start = column_index * q_dev
    local_out, local_lse = self_attend(passage_qkv)
    pool_q, pool_out, pool_resid, pool_student = (
        lax.all_gather(passage_qkv[:, 0], "pb", axis=0, tiled=True),
        lax.all_gather(local_out, "pb", axis=0, tiled=True),
        lax.all_gather(passage_resid, "pb", axis=0, tiled=True),
        lax.all_gather(student_passage, "pb", axis=0, tiled=True),
    )
    pool_lse = lax.all_gather(local_lse, "pb", axis=0, tiled=True)
    row_kv, row_student = (
        lax.all_gather(query_kv, "pa", axis=0, tiled=True),
        lax.all_gather(student_query, "pa", axis=0, tiled=True),
    )
    holder = block_holder[:, :, 0].reshape(-1)
    total_rows = holder.shape[0]
    is_mine = (holder == column_index).astype(jnp.int32)
    slot_place = jnp.cumsum(is_mine) - 1
    slot_pick = (slot_place[None, :] == jnp.arange(HOLD_CAP, dtype=jnp.int32)[:, None]) & (
        is_mine[None, :] == 1
    )
    block_index = jnp.arange(total_rows, dtype=jnp.int32)
    slot_block = jnp.sum(jnp.where(slot_pick, block_index[None, :], 0), axis=1)
    slot_live = jnp.any(slot_pick, axis=1)
    slot_query = slot_block // blocks
    slot_part = slot_block % blocks
    slot_local = cand_local.reshape(total_rows, slot_len)[slot_block]
    slot_column = jnp.arange(slot_len, dtype=jnp.int32)
    slot_valid = slot_live[:, None] & (
        slot_part[:, None] * slot_len + slot_column[None, :] < counts[slot_query][:, None]
    )

    def one_slot(slot_item):
        query_row, pool_rows = slot_item
        teacher = score_block(
            pool_q[pool_rows],
            pool_out[pool_rows],
            pool_lse[pool_rows],
            pool_resid[pool_rows],
            row_kv[query_row],
            weights,
        )
        student = student_scale * jnp.dot(
            pool_student[pool_rows], row_student[query_row], preferred_element_type=jnp.float32
        )
        return (teacher, student)

    slot_teacher, slot_student = lax.map(one_slot, (slot_query, slot_local))
    slot_teacher = jnp.where(slot_valid, slot_teacher, jnp.float32(0.0))
    slot_student = jnp.where(slot_valid, slot_student, jnp.float32(0.0))
    pick_matrix = slot_pick.astype(jnp.float32)
    teacher_table = jnp.dot(pick_matrix.T, slot_teacher, precision=highest).reshape(
        group_rows, blocks * slot_len
    )
    student_table = jnp.dot(pick_matrix.T, slot_student, precision=highest).reshape(
        group_rows, blocks * slot_len
    )
    teacher_all, student_all = lax.psum((teacher_table, student_table), "pa")
    row_valid = jnp.arange(blocks * slot_len, dtype=jnp.int32)[None, :] < counts[:, None]
    loss_all, grad_rows = distill(teacher_all, student_all, row_valid)
    own_teacher = lax.dynamic_slice_in_dim(teacher_all, row_start, q_dev, 0)
    own_valid = lax.dynamic_slice_in_dim(row_valid, row_start, q_dev, 0)
    query_loss = lax.dynamic_slice_in_dim(loss_all, row_start, q_dev, 0)
    teacher_scores = jnp.where(own_valid, own_teacher, jnp.float32(0.0))
    slot_grad = jnp.dot(pick_matrix, grad_rows.reshape(total_rows, slot_len), precision=highest)
    cand_student = pool_student[slot_local].astype(jnp.float32)
    query_term = student_scale * jnp.einsum(
        "sc,scd->sd", slot_grad, cand_student, precision=highest
    )
    owner_pick = (
        (slot_query[:, None] == jnp.arange(group_rows, dtype=jnp.int32)[None, :])
        & slot_live[:, None]
    ).astype(jnp.float32)
    query_table = jnp.dot(owner_pick.T, query_term, precision=highest)
    grad_query = lax.psum_scatter(query_table, "pa", scatter_dimension=0, tiled=True)
    pool_size = pool_student.shape[0]
    pool_hit = (
        slot_local[:, :, None] == jnp.arange(pool_size, dtype=jnp.int32)[None, None, :]
    ).astype(jnp.float32)
    pool_weight = jnp.einsum("sc,scp->ps", slot_grad, pool_hit, precision=highest)
    slot_embed = row_student[slot_query].astype(jnp.float32)
    pool_table = student_scale * jnp.dot(pool_weight, slot_embed, precision=highest)
    grad_passage = lax.psum_scatter(pool_table, "pb", scatter_dimension=0, tiled=True)
    return (teacher_scores, query_loss, grad_query, grad_passage)


def solution(mesh):
    placed = (
        P(("pb", "pa"), None, None, None),
        P(("pb", "pa"), None),
        P("pb", None, None),
        P("pb", None, None),
        P("pb"),
        P(("pa", "pb"), None, None, None),
        P(("pa", "pb"), None),
        P(("pa", "pb"), None),
        P(),
        P(),
        P(),
        P(),
        P(),
        P(),
    )
    return jax.shard_map(
        local,
        mesh=mesh,
        in_specs=placed,
        out_specs=(
            P(("pb", "pa"), None),
            P(("pb", "pa")),
            P(("pb", "pa"), None),
            P(("pa", "pb"), None),
        ),
        check_vma=False,
    )
```

profile of v0, /device:TPU:0, one launch (start us, length us, event | category | flops | bytes accessed | tf_op | source)
XLA Modules:
  0.0 351.1 jit_solution(4080465376627700940)
XLA Ops:
  7.2 4.1 %reshape.286 = bf16[8,3,32,16,64]{4,3,2,1,0:T(8,128)(2,1)S(1)} reshape(bf16[8,3,32,1024]{3,2,1,0:T(8,128)(2,1)} %param.21) | data formatting | bytes 3145728 | tf_op jit(solution)/shard_map/reshape | solution.py:17
  16.3 1.9 slice.22
  18.9 14.8 %all-gather.1 = bf16[4,1,1024]{2,1,0:T(2,128)(2,1)S(1)} all-gather(bf16[1,1,1024]{2,1,0:T(2,128)(2,1)S(1)} %bitcast.167), channel_id=1, replica_groups=mesh['pb'=8,'pa'=4] {'pa'}, dimensions={0}, use_global_device_ids=true | all-gather | bytes 10240 | tf_op jit(solution)/shard_map/all_gather | solution.py:123
  37.9 9.4 %all_gather.26 = bf16[64,1024]{1,0:T(8,128)(2,1)S(1)} all-gather(bf16[8,1024]{1,0:T(8,128)(2,1)S(1)} %copy-done.10), channel_id=1, replica_groups=mesh['pb'=8,'pa'=4] {'pb'}, dimensions={0}, use_global_device_ids=true | all-gather | bytes 147456 | tf_op jit(solution)/shard_map/all_gather | solution.py:118
  48.9 11.5 %all_gather.22 = f32[64,16,32]{2,1,0:T(8,128)} all-gather(f32[8,16,32]{2,1,0:T(8,128)S(1)} %log_add_fusion.1), channel_id=1, replica_groups=mesh['pb'=8,'pa'=4] {'pb'}, dimensions={0}, use_global_device_ids=true | all-gather | bytes 147456 | tf_op jit(solution)/shard_map/all_gather | solution.py:120
  60.4 8.4 %all_gather.25 = bf16[64,1024]{1,0:T(8,128)(2,1)S(1)} all-gather(bf16[8,1024]{1,0:T(8,128)(2,1)S(1)} %copy-done.11), channel_id=1, replica_groups=mesh['pb'=8,'pa'=4] {'pb'}, dimensions={0}, use_global_device_ids=true | all-gather | bytes 147456 | tf_op jit(solution)/shard_map/all_gather | solution.py:117
  68.8 16.5 %all_gather.21 = bf16[4,2,32,1024]{3,2,1,0:T(8,128)(2,1)} all-gather(bf16[1,2,32,1024]{3,2,1,0:T(8,128)(2,1)S(1)} %copy-done.5), channel_id=1, replica_groups=mesh['pb'=8,'pa'=4] {'pa'}, dimensions={0}, use_global_device_ids=true | all-gather | bytes 655360 | tf_op jit(solution)/shard_map/all_gather | solution.py:122
  86.4 9.2 %all-gather.7.cloned.1.call-done = bf16[64,1,32,1024]{3,2,1,0:T(8,128)(2,1)} async-done(((bf16[8,1,32,1024]{3,2,1,0:T(8,128)(2,1)}), bf16[64,1,32,1024]{3,2,1,0:T(8,128)(2,1)}) %all-gather.7.cloned.1.call-update) | async-done | bytes 4194320 | tf_op jit(solution)/shard_map/all_gather | solution.py:115
  95.6 200.7 %while.13 = (s32[]{:T(128)}, f32[4,32]{1,0:T(4,128)}, f32[4,32]{1,0:T(4,128)}, s32[4]{0:T(128)}, bf16[4,2,32,1024]{3,2,1,0:T(8,128)(2,1)}, /*index=5*/s32[4,32]{...) while((s32[]{:T(128)}, f32[4,32]{1,0:T(4,128)}, ...), condition=%wide.region_12.13_spmd.clone, body=%wide.region_5.12_spmd.sunk.clone | while | flops 211534976 | bytes 60472692 | solution.py:158
  99.9 2.9 gather_fusion.3
  102.8 4.0 %reshape.416 = bf16[1024,16,64]{2,1,0:T(8,128)(2,1)} reshape(bf16[32,32,1024]{2,1,0:T(8,128)(2,1)S(1)} %gather_fusion.3) | data formatting | bytes 4194304 | tf_op jit(solution)/shard_map/while/body/eval_jaxpr/reshape | solution.py:37
  106.8 4.6 %multiply_reduce_fusion.7 = (f32[16,1024]{1,0:T(8,128)S(1)}, f32[16,32,1024]{2,1,0:T(8,128)S(1)}) fusion(bf16[1024,16,64]{2,1,0:T(8,128)(2,1)} %reshape.416, bf16[32,16,64]{2,1,0:T(8,128)(2,1)S(1)} %squeeze.39), kind=kOutput, calls=%fused_computation.15.clone.1.clone | convolution fusion | flops 68141056 | bytes 4325376 | tf_op jit(solution)/shard_map/while/body/eval_jaxpr/rhd,ahd->har/dot_general | solution.py:40
  113.8 1.8 multiply_divide_fusion.3
  115.6 6.5 %reshape.417 = f32[16,32,32,32]{3,2,1,0:T(8,128)} reshape(f32[16,32,1024]{2,1,0:T(8,128)} %multiply_divide_fusion.3) | data formatting | bytes 4194304 | tf_op jit(solution)/shard_map/while/body/eval_jaxpr/reshape | solution.py:51
  122.1 5.6 %reduce_sum.121 = f32[16,32,32]{2,1,0:T(8,128)S(1)} reduce(f32[16,32,32,32]{3,2,1,0:T(8,128)} %reshape.417, f32[]{:T(128)} %constant.91.clone.1..sunk.1), dimensions={3}, to_apply=%region_8.8 | reduce | flops 507904 | bytes 2162692 | tf_op jit(solution)/shard_map/while/body/eval_jaxpr/reduce_sum | solution.py:51
  128.2 3.0 gather_fusion.1
  131.2 4.0 %reshape.414 = bf16[32,32,16,64]{3,2,1,0:T(8,128)(2,1)} reshape(bf16[32,32,1024]{2,1,0:T(8,128)(2,1)S(1)} %gather_fusion.1) | data formatting | bytes 4194304 | tf_op jit(solution)/shard_map/while/body/eval_jaxpr/reshape | solution.py:57
  135.2 3.5 %fusion.131 = f32[32,16,1,64]{3,2,1,0:T(1,128)S(1)} fusion(bf16[32,32,16,64]{3,2,1,0:T(8,128)(2,1)} %reshape.414, bf16[16,32,32,1]{2,0,1,3:T(8,128)(2,1)S(1)} %fusion.130), kind=kOutput, calls=%fused_computation.9.clone.1.clone | convolution fusion | flops 2097152 | bytes 2260992 | tf_op jit(solution)/shard_map/while/body/eval_jaxpr/hbt,bthd->bhd/dot_general | solution.py:58
  150.1 2.9 gather_fusion.3
  153.0 4.0 %reshape.416 = bf16[1024,16,64]{2,1,0:T(8,128)(2,1)} reshape(bf16[32,32,1024]{2,1,0:T(8,128)(2,1)S(1)} %gather_fusion.3) | data formatting | bytes 4194304 | tf_op jit(solution)/shard_map/while/body/eval_jaxpr/reshape | solution.py:37
  157.0 4.6 %multiply_reduce_fusion.7 = (f32[16,1024]{1,0:T(8,128)S(1)}, f32[16,32,1024]{2,1,0:T(8,128)S(1)}) fusion(bf16[1024,16,64]{2,1,0:T(8,128)(2,1)} %reshape.416, bf16[32,16,64]{2,1,0:T(8,128)(2,1)S(1)} %squeeze.39), kind=kOutput, calls=%fused_computation.15.clone.1.clone | convolution fusion | flops 68141056 | bytes 4325376 | tf_op jit(solution)/shard_map/while/body/eval_jaxpr/rhd,ahd->har/dot_general | solution.py:40
  164.0 1.8 multiply_divide_fusion.3
  165.8 6.5 %reshape.417 = f32[16,32,32,32]{3,2,1,0:T(8,128)} reshape(f32[16,32,1024]{2,1,0:T(8,128)} %multiply_divide_fusion.3) | data formatting | bytes 4194304 | tf_op jit(solution)/shard_map/while/body/eval_jaxpr/reshape | solution.py:51
  172.2 5.6 %reduce_sum.121 = f32[16,32,32]{2,1,0:T(8,128)S(1)} reduce(f32[16,32,32,32]{3,2,1,0:T(8,128)} %reshape.417, f32[]{:T(128)} %constant.91.clone.1..sunk.1), dimensions={3}, to_apply=%region_8.8 | reduce | flops 507904 | bytes 2162692 | tf_op jit(solution)/shard_map/while/body/eval_jaxpr/reduce_sum | solution.py:51
  178.4 3.0 gather_fusion.1
  181.4 4.0 %reshape.414 = bf16[32,32,16,64]{3,2,1,0:T(8,128)(2,1)} reshape(bf16[32,32,1024]{2,1,0:T(8,128)(2,1)S(1)} %gather_fusion.1) | data formatting | bytes 4194304 | tf_op jit(solution)/shard_map/while/body/eval_jaxpr/reshape | solution.py:57
  185.4 3.5 %fusion.131 = f32[32,16,1,64]{3,2,1,0:T(1,128)S(1)} fusion(bf16[32,32,16,64]{3,2,1,0:T(8,128)(2,1)} %reshape.414, bf16[16,32,32,1]{2,0,1,3:T(8,128)(2,1)S(1)} %fusion.130), kind=kOutput, calls=%fused_computation.9.clone.1.clone | convolution fusion | flops 2097152 | bytes 2260992 | tf_op jit(solution)/shard_map/while/body/eval_jaxpr/hbt,bthd->bhd/dot_general | solution.py:58
  200.3 2.9 gather_fusion.3
  203.1 4.0 %reshape.416 = bf16[1024,16,64]{2,1,0:T(8,128)(2,1)} reshape(bf16[32,32,1024]{2,1,0:T(8,128)(2,1)S(1)} %gather_fusion.3) | data formatting | bytes 4194304 | tf_op jit(solution)/shard_map/while/body/eval_jaxpr/reshape | solution.py:37
  207.2 4.6 %multiply_reduce_fusion.7 = (f32[16,1024]{1,0:T(8,128)S(1)}, f32[16,32,1024]{2,1,0:T(8,128)S(1)}) fusion(bf16[1024,16,64]{2,1,0:T(8,128)(2,1)} %reshape.416, bf16[32,16,64]{2,1,0:T(8,128)(2,1)S(1)} %squeeze.39), kind=kOutput, calls=%fused_computation.15.clone.1.clone | convolution fusion | flops 68141056 | bytes 4325376 | tf_op jit(solution)/shard_map/while/body/eval_jaxpr/rhd,ahd->har/dot_general | solution.py:40
  214.1 1.8 multiply_divide_fusion.3
  215.9 6.5 %reshape.417 = f32[16,32,32,32]{3,2,1,0:T(8,128)} reshape(f32[16,32,1024]{2,1,0:T(8,128)} %multiply_divide_fusion.3) | data formatting | bytes 4194304 | tf_op jit(solution)/shard_map/while/body/eval_jaxpr/reshape | solution.py:51
  222.4 5.6 %reduce_sum.121 = f32[16,32,32]{2,1,0:T(8,128)S(1)} reduce(f32[16,32,32,32]{3,2,1,0:T(8,128)} %reshape.417, f32[]{:T(128)} %constant.91.clone.1..sunk.1), dimensions={3}, to_apply=%region_8.8 | reduce | flops 507904 | bytes 2162692 | tf_op jit(solution)/shard_map/while/body/eval_jaxpr/reduce_sum | solution.py:51
  228.5 3.0 gather_fusion.1
  231.5 4.0 %reshape.414 = bf16[32,32,16,64]{3,2,1,0:T(8,128)(2,1)} reshape(bf16[32,32,1024]{2,1,0:T(8,128)(2,1)S(1)} %gather_fusion.1) | data formatting | bytes 4194304 | tf_op jit(solution)/shard_map/while/body/eval_jaxpr/reshape | solution.py:57
  235.5 3.5 %fusion.131 = f32[32,16,1,64]{3,2,1,0:T(1,128)S(1)} fusion(bf16[32,32,16,64]{3,2,1,0:T(8,128)(2,1)} %reshape.414, bf16[16,32,32,1]{2,0,1,3:T(8,128)(2,1)S(1)} %fusion.130), kind=kOutput, calls=%fused_computation.9.clone.1.clone | convolution fusion | flops 2097152 | bytes 2260992 | tf_op jit(solution)/shard_map/while/body/eval_jaxpr/hbt,bthd->bhd/dot_general | solution.py:58
  250.4 2.9 gather_fusion.3
  253.3 4.0 %reshape.416 = bf16[1024,16,64]{2,1,0:T(8,128)(2,1)} reshape(bf16[32,32,1024]{2,1,0:T(8,128)(2,1)S(1)} %gather_fusion.3) | data formatting | bytes 4194304 | tf_op jit(solution)/shard_map/while/body/eval_jaxpr/reshape | solution.py:37
  257.3 4.6 %multiply_reduce_fusion.7 = (f32[16,1024]{1,0:T(8,128)S(1)}, f32[16,32,1024]{2,1,0:T(8,128)S(1)}) fusion(bf16[1024,16,64]{2,1,0:T(8,128)(2,1)} %reshape.416, bf16[32,16,64]{2,1,0:T(8,128)(2,1)S(1)} %squeeze.39), kind=kOutput, calls=%fused_computation.15.clone.1.clone | convolution fusion | flops 68141056 | bytes 4325376 | tf_op jit(solution)/shard_map/while/body/eval_jaxpr/rhd,ahd->har/dot_general | solution.py:40
  264.3 1.8 multiply_divide_fusion.3
  266.1 6.5 %reshape.417 = f32[16,32,32,32]{3,2,1,0:T(8,128)} reshape(f32[16,32,1024]{2,1,0:T(8,128)} %multiply_divide_fusion.3) | data formatting | bytes 4194304 | tf_op jit(solution)/shard_map/while/body/eval_jaxpr/reshape | solution.py:51
  272.6 5.6 %reduce_sum.121 = f32[16,32,32]{2,1,0:T(8,128)S(1)} reduce(f32[16,32,32,32]{3,2,1,0:T(8,128)} %reshape.417, f32[]{:T(128)} %constant.91.clone.1..sunk.1), dimensions={3}, to_apply=%region_8.8 | reduce | flops 507904 | bytes 2162692 | tf_op jit(solution)/shard_map/while/body/eval_jaxpr/reduce_sum | solution.py:51
  278.7 3.0 gather_fusion.1
  281.7 4.0 %reshape.414 = bf16[32,32,16,64]{3,2,1,0:T(8,128)(2,1)} reshape(bf16[32,32,1024]{2,1,0:T(8,128)(2,1)S(1)} %gather_fusion.1) | data formatting | bytes 4194304 | tf_op jit(solution)/shard_map/while/body/eval_jaxpr/reshape | solution.py:57
  285.7 3.5 %fusion.131 = f32[32,16,1,64]{3,2,1,0:T(1,128)S(1)} fusion(bf16[32,32,16,64]{3,2,1,0:T(8,128)(2,1)} %reshape.414, bf16[16,32,32,1]{2,0,1,3:T(8,128)(2,1)S(1)} %fusion.130), kind=kOutput, calls=%fused_computation.9.clone.1.clone | convolution fusion | flops 2097152 | bytes 2260992 | tf_op jit(solution)/shard_map/while/body/eval_jaxpr/hbt,bthd->bhd/dot_general | solution.py:58
  298.2 11.7 %all-reduce.1 = (f32[4,64]{1,0:T(4,128)S(1)}, f32[4,64]{1,0:T(4,128)S(1)}) all-reduce(f32[4,64]{1,0:T(4,128)S(1)} %reshape.287, f32[4,64]{1,0:T(4,128)S(1)} %reshape.288), channel_id=1, replica_groups=mesh['pb'=8,'pa'=4] {'pa'}, use_global_device_ids=true, to_apply=%region_13.14 | all-reduce | flops 512 | bytes 4096 | tf_op jit(solution)/shard_map/psum | solution.py:168
  315.3 15.5 %all-reduce = f32[4,1024]{1,0:T(4,128)S(1)} all-reduce(f32[4,1024]{1,0:T(4,128)S(1)} %fusion.38), channel_id=3, replica_groups=mesh['pb'=8,'pa'=4] {'pa'}, use_global_device_ids=true, to_apply=%region_20.21.clone | all-reduce | flops 4096 | bytes 32768
  333.2 11.3 %reduce-scatter.2.cloned.1.call-done = f32[8,1024]{1,0:T(8,128)} async-done(((f32[64,1024]{1,0:T(8,128)}), f32[8,1024]{1,0:T(8,128)}) %reduce-scatter.2.cloned.1.call-update) | async-done | bytes 32784 | tf_op jit(solution)/shard_map/reduce_scatter | solution.py:193
  (256 shorter events, 70.5 us)
Async XLA Ops:
  7.2 30.1 %copy-start = (s32[4,2,32]{2,1,0:T(2,128)S(1)}, s32[4,2,32]{2,1,0:T(2,128)}, u32[]{:S(2)}) copy-start(s32[4,2,32]{2,1,0:T(2,128)} %param.19) | copy-start | bytes 3076
  7.2 79.2 %all-gather.5.cloned.1.call-start = ((), (), s32[]{:S(2)}) async-start(), calls=%async_computation.1 | async-start | bytes 4718592 | tf_op jit(solution)/shard_map/all_gather | solution.py:116
  14.7 3.7 %copy-start.16 = (s32[4,2,1]{0,2,1:T(1,128)S(1)}, s32[4,2,1]{0,2,1:T(1,128)}, u32[]{:S(2)}) copy-start(s32[4,2,1]{0,2,1:T(1,128)} %param.18) | copy-start | bytes 100
  14.7 4.2 %copy-start.14 = (bf16[1,1024]{1,0:T(2,128)(2,1)S(1)}, bf16[1,1024]{1,0:T(2,128)(2,1)}, u32[]{:S(2)}) copy-start(bf16[1,1024]{1,0:T(2,128)(2,1)} %param.17) | copy-start | bytes 6148
  14.7 20.2 %copy-start.1 = (s32[4]{0:T(128)S(1)}, s32[4]{0:T(128)}, u32[]{:S(2)}) copy-start(s32[4]{0:T(128)} %param.20) | copy-start | bytes 52
  14.7 23.2 %copy-start.10 = (bf16[8,1024]{1,0:T(8,128)(2,1)S(1)}, bf16[8,1024]{1,0:T(8,128)(2,1)}, u32[]{:S(2)}) copy-start(bf16[8,1024]{1,0:T(8,128)(2,1)} %param.23) | copy-start | bytes 49156
  16.2 79.4 %all-gather.7.cloned.1.call-start = ((), (), s32[]{:S(2)}) async-start(), calls=%async_computation.3 | async-start | bytes 4718592 | tf_op jit(solution)/shard_map/all_gather | solution.py:115
  18.2 30.0 %copy-start.17 = (u32[32]{0:T(128)S(1)}, u32[32]{0:T(128)}, u32[]{:S(2)}) copy-start(u32[32]{0:T(128)} %constant.107) | copy-start | bytes 388
  18.2 42.2 %copy-start.11 = (bf16[8,1024]{1,0:T(8,128)(2,1)S(1)}, bf16[8,1024]{1,0:T(8,128)(2,1)}, u32[]{:S(2)}) copy-start(bf16[8,1024]{1,0:T(8,128)(2,1)} %param.22) | copy-start | bytes 49156
  18.2 326.4 %reduce-scatter.2.cloned.1.call-start = ((), (), s32[]{:S(2)}) async-start(), calls=%async_computation.2 | async-start | bytes 294912 | tf_op jit(solution)/shard_map/reduce_scatter | solution.py:193
  18.3 50.5 %copy-start.5 = (bf16[1,2,32,1024]{3,2,1,0:T(8,128)(2,1)S(1)}, bf16[1,2,32,1024]{3,2,1,0:T(8,128)(2,1)}, u32[]{:S(2)}) copy-start(bf16[1,2,32,1024]{3,2,1,0:T(8,128)(2,1)} %param.16) | copy-start | bytes 393220
  34.3 0.6 copy-start.15
  95.6 7.2 %copy-start.12 = (s32[4,32]{1,0:T(4,128)}, s32[4,32]{1,0:T(4,128)S(1)}, u32[]{:S(2)}) copy-start(s32[4,32]{1,0:T(4,128)S(1)} %get-tuple-element.378) | copy-start | bytes 1540 | tf_op jit(solution)/shard_map/while
  99.9 12.0 %copy-start.4 = (s32[1024]{0:T(1024)}, s32[1024]{0:T(1024)S(1)}, u32[]{:S(2)}) copy-start(s32[1024]{0:T(1024)S(1)} %pad_clamp_fusion.6) | copy-start | bytes 12292 | tf_op jit(solution)/shard_map/while
  135.2 5.0 %copy-start.2 = (bf16[1024,1024]{1,0:T(8,128)(2,1)S(1)}, bf16[1024,1024]{1,0:T(8,128)(2,1)}, u32[]{:S(2)}) copy-start(bf16[1024,1024]{1,0:T(8,128)(2,1)} %get-tuple-element.382) | copy-start | bytes 6291460 | tf_op jit(solution)/shard_map/while
  138.9 2.1 copy-start.6
  138.9 2.1 copy-start.7
  138.9 2.1 copy-start.8
  138.9 2.1 copy-start.9
  140.2 1.6 copy-start.3
  140.7 5.0 %copy-start.13 = (s32[4,32]{1,0:T(4,128)S(1)}, s32[4,32]{1,0:T(4,128)}, u32[]{:S(2)}) copy-start(s32[4,32]{1,0:T(4,128)} %copy-done.12) | copy-start | bytes 1540 | tf_op jit(solution)/shard_map/while
  145.8 7.2 %copy-start.12 = (s32[4,32]{1,0:T(4,128)}, s32[4,32]{1,0:T(4,128)S(1)}, u32[]{:S(2)}) copy-start(s32[4,32]{1,0:T(4,128)S(1)} %get-tuple-element.378) | copy-start | bytes 1540 | tf_op jit(solution)/shard_map/while
  150.1 12.0 %copy-start.4 = (s32[1024]{0:T(1024)}, s32[1024]{0:T(1024)S(1)}, u32[]{:S(2)}) copy-start(s32[1024]{0:T(1024)S(1)} %pad_clamp_fusion.6) | copy-start | bytes 12292 | tf_op jit(solution)/shard_map/while
  185.4 5.0 %copy-start.2 = (bf16[1024,1024]{1,0:T(8,128)(2,1)S(1)}, bf16[1024,1024]{1,0:T(8,128)(2,1)}, u32[]{:S(2)}) copy-start(bf16[1024,1024]{1,0:T(8,128)(2,1)} %get-tuple-element.382) | copy-start | bytes 6291460 | tf_op jit(solution)/shard_map/while
  189.1 2.1 copy-start.6
  189.1 2.1 copy-start.7
  189.1 2.1 copy-start.8
  189.1 2.1 copy-start.9
  190.3 1.6 copy-start.3
  190.9 5.0 %copy-start.13 = (s32[4,32]{1,0:T(4,128)S(1)}, s32[4,32]{1,0:T(4,128)}, u32[]{:S(2)}) copy-start(s32[4,32]{1,0:T(4,128)} %copy-done.12) | copy-start | bytes 1540 | tf_op jit(solution)/shard_map/while
  196.0 7.2 %copy-start.12 = (s32[4,32]{1,0:T(4,128)}, s32[4,32]{1,0:T(4,128)S(1)}, u32[]{:S(2)}) copy-start(s32[4,32]{1,0:T(4,128)S(1)} %get-tuple-element.378) | copy-start | bytes 1540 | tf_op jit(solution)/shard_map/while
  200.2 12.0 %copy-start.4 = (s32[1024]{0:T(1024)}, s32[1024]{0:T(1024)S(1)}, u32[]{:S(2)}) copy-start(s32[1024]{0:T(1024)S(1)} %pad_clamp_fusion.6) | copy-start | bytes 12292 | tf_op jit(solution)/shard_map/while
  235.5 5.0 %copy-start.2 = (bf16[1024,1024]{1,0:T(8,128)(2,1)S(1)}, bf16[1024,1024]{1,0:T(8,128)(2,1)}, u32[]{:S(2)}) copy-start(bf16[1024,1024]{1,0:T(8,128)(2,1)} %get-tuple-element.382) | copy-start | bytes 6291460 | tf_op jit(solution)/shard_map/while
  239.2 2.1 copy-start.6
  239.2 2.1 copy-start.7
  239.3 2.1 copy-start.8
  239.3 2.1 copy-start.9
  240.5 1.6 copy-start.3
  241.1 5.0 %copy-start.13 = (s32[4,32]{1,0:T(4,128)S(1)}, s32[4,32]{1,0:T(4,128)}, u32[]{:S(2)}) copy-start(s32[4,32]{1,0:T(4,128)} %copy-done.12) | copy-start | bytes 1540 | tf_op jit(solution)/shard_map/while
  246.1 7.2 %copy-start.12 = (s32[4,32]{1,0:T(4,128)}, s32[4,32]{1,0:T(4,128)S(1)}, u32[]{:S(2)}) copy-start(s32[4,32]{1,0:T(4,128)S(1)} %get-tuple-element.378) | copy-start | bytes 1540 | tf_op jit(solution)/shard_map/while
  250.4 12.0 %copy-start.4 = (s32[1024]{0:T(1024)}, s32[1024]{0:T(1024)S(1)}, u32[]{:S(2)}) copy-start(s32[1024]{0:T(1024)S(1)} %pad_clamp_fusion.6) | copy-start | bytes 12292 | tf_op jit(solution)/shard_map/while
  285.7 5.0 %copy-start.2 = (bf16[1024,1024]{1,0:T(8,128)(2,1)S(1)}, bf16[1024,1024]{1,0:T(8,128)(2,1)}, u32[]{:S(2)}) copy-start(bf16[1024,1024]{1,0:T(8,128)(2,1)} %get-tuple-element.382) | copy-start | bytes 6291460 | tf_op jit(solution)/shard_map/while
  289.4 2.1 copy-start.6
  289.4 2.1 copy-start.7
  289.4 2.1 copy-start.8
  289.4 2.1 copy-start.9
  290.6 1.6 copy-start.3
  291.2 5.0 %copy-start.13 = (s32[4,32]{1,0:T(4,128)S(1)}, s32[4,32]{1,0:T(4,128)}, u32[]{:S(2)}) copy-start(s32[4,32]{1,0:T(4,128)} %copy-done.12) | copy-start | bytes 1540 | tf_op jit(solution)/shard_map/while
Sparse Core Ops, SparseCore 0:
  16.4 40.5 all-gather.4
  58.9 36.6 all-gather.6
  313.7 30.8 reduce-scatter.1
where the time goes:
time: 354 us; the launch traced here: 351 us
  local copies, waits for them, and re-layouts  135 us (38%)
  blocking collectives  87.8 us (25%)
  matrix products  45.9 us (13%)
  other arithmetic  38.9 us (11%)
  waiting for transfers between devices  20.6 us (6%)
  between operations  14 us (4%)
  loops' own time  8.72 us (2%)
    reshape x4, local copies, waits for them, and re-layouts, score_block(): spread.reshape(HEADS, query_len, passage_count, length)  25.8 us
    reduce_sum x4, other arithmetic, score_block(): jnp.sum(spread.reshape(HEADS, query_len, passage_count, length), axis=3)  22.5 us
    dot_general x4, matrix products, score_block(): jnp.einsum('rhd,ahd->har', token_rows, key_rows, preferred_element_type=j...  18.3 us
    all_gather x1, blocking collectives, local(): lax.all_gather(query_kv, 'pa', axis=0, tiled=True)  16.5 us
    reshape x4, local copies, waits for them, and re-layouts, score_block(): self_rows = pass_o.reshape(passage_count, length, HEADS, head_dim)  16.1 us
    reshape x4, local copies, waits for them, and re-layouts, score_block(): token_rows = pass_q.reshape(passage_count * length, HEADS, head_dim)  16.1 us
    unnamed x1, blocking collectives  15.5 us
    all_gather x1, blocking collectives, local(): lax.all_gather(student_query, 'pa', axis=0, tiled=True)  14.8 us
  transfers between devices with their start and end apart: 3, of which 2 were waited for; matrix products, arithmetic and copies ran while one was open for 4% of the time, Pallas kernels for 0%

commit v1 on v0

v1 whole, which is shorter than its diff:
```python
import functools

import jax
import jax.numpy as jnp
from jax import lax
from jax.experimental import pallas as pl
from jax.experimental.pallas import tpu as pltpu
from jax.sharding import PartitionSpec as P

HEADS = 16
HEAD_DIM = 64
PAIRS = HEADS // 2
LANES = 128
student_scale = 0.125
norm_eps = 1e-05
VMEM_LIMIT = 56 * 1024 * 1024
NT = (((1,), (1,)), ((), ()))


def iota(shape, axis):
    return lax.broadcasted_iota(jnp.int32, shape, axis)


def pair_masks(rows):
    low = iota((rows, LANES), 1) < HEAD_DIM
    return low, jnp.logical_not(low)


def self_kernel(qkv_ref, out_ref, lse_ref):
    passages, _, length, _ = qkv_ref.shape
    rows = passages * length
    masks = pair_masks(rows)
    same = iota((rows, rows), 0) // length == iota((rows, rows), 1) // length

    def body(k, carry):
        lanes = pl.ds(pl.multiple_of(k * LANES, LANES), LANES)
        q = qkv_ref[:, 0, :, lanes].reshape(rows, LANES)
        key = qkv_ref[:, 1, :, lanes].reshape(rows, LANES)
        value = qkv_ref[:, 2, :, lanes].reshape(rows, LANES)
        outs, lses = [], []
        for mask in masks:
            q_head = jnp.where(mask, q.astype(jnp.float32) * 0.125, 0.0).astype(jnp.bfloat16)
            scores = lax.dot_general(key, q_head, NT, preferred_element_type=jnp.float32)
            scores = jnp.where(same, scores, -1e30)
            top = jnp.max(scores, axis=0, keepdims=True)
            scaled = jnp.exp(scores - top)
            total = jnp.sum(scaled, axis=0, keepdims=True)
            lses.append(top + jnp.log(total))
            probs = (scaled / total).T.astype(jnp.bfloat16)
            outs.append(jnp.dot(probs, value, preferred_element_type=jnp.float32))
        out_ref[:, lanes] = jnp.where(masks[0], outs[0], outs[1]).astype(jnp.bfloat16)
        lse_ref[k] = jnp.concatenate(lses, axis=0)
        return carry

    lax.fori_loop(0, PAIRS, body, 0)


def cross_kernel(k_ref, q_ref, so_ref, lse_ref, kwt_ref, part_ref):
    queries, keys, _ = k_ref.shape
    passages, _, length, _ = q_ref.shape
    rows = passages * length
    masks = pair_masks(rows)
    out_low = iota((queries * passages, LANES), 1) < HEAD_DIM
    own = (iota((passages, rows), 1) // length == iota((passages, rows), 0)).astype(jnp.float32)
    spots = [
        jnp.where(iota((rows, LANES), 1) == iota((rows, LANES), 0) // length + h * passages, 1.0 / length, 0.0).astype(
            jnp.bfloat16
        )
        for h in range(2)
    ]

    def body(k, carry):
        lanes = pl.ds(pl.multiple_of(k * LANES, LANES), LANES)
        q = q_ref[:, 0, :, lanes].reshape(rows, LANES)
        key = k_ref[:, :, lanes].reshape(queries * keys, LANES)
        so = so_ref[:, lanes]
        lse = lse_ref[k]
        weights, parts = None, []
        for h in range(2):
            q_head = jnp.where(masks[h], q.astype(jnp.float32) * 0.125, 0.0).astype(jnp.bfloat16)
            scores = lax.dot_general(key, q_head, NT, preferred_element_type=jnp.float32)
            scores = scores.reshape(queries, keys, rows)
            self_lse = lse[h : h + 1]
            top = jnp.maximum(jnp.max(scores, axis=1), self_lse)
            scaled = jnp.exp(scores - top[:, None, :])
            self_term = jnp.exp(self_lse - top)
            inverse = 1.0 / (jnp.sum(scaled, axis=1) + self_term)
            spread = (scaled * inverse[:, None, :]).reshape(queries * keys, rows).astype(jnp.bfloat16)
            weight = jnp.dot(spread, spots[h], preferred_element_type=jnp.float32)
            weights = weight if weights is None else weights + weight
            token = self_term * inverse * (1.0 / length)
            token = (token[:, None, :] * own[None]).reshape(queries * passages, rows).astype(jnp.bfloat16)
            parts.append(jnp.dot(token, so, preferred_element_type=jnp.float32))
        part_ref[:, lanes] = jnp.where(out_low, parts[0], parts[1])
        kwt_ref[k] = weights.T[: 2 * passages].astype(jnp.bfloat16)
        return carry

    lax.fori_loop(0, PAIRS, body, 0)


def head_kernel(v_ref, kwt_ref, part_ref, resid_ref, wo_ref, gain_ref, bias_ref, wd_ref, bd_ref, out_w_ref, teacher_ref, pooled, table):
    step = pl.program_id(0)
    queries, keys, width = v_ref.shape
    passages = resid_ref.shape[0]
    group = 8
    cols = group * keys
    span = 2 * passages
    own = (iota((group, span, cols), 2) // keys == iota((group, span, cols), 0)).astype(jnp.float32)
    low = iota((group, passages, LANES), 2) < HEAD_DIM

    def body(k, carry):
        lanes = pl.ds(pl.multiple_of(k * LANES, LANES), LANES)
        for c in range(queries // group):
            weight = kwt_ref[k, :, c * cols : (c + 1) * cols].astype(jnp.float32)
            weight = (weight[None] * own).reshape(group * span, cols).astype(jnp.bfloat16)
            value = v_ref[c * group : (c + 1) * group, :, lanes].reshape(cols, LANES)
            got = jnp.dot(weight, value, preferred_element_type=jnp.float32)
            got = got.reshape(group, 2, passages, LANES)
            got = jnp.where(low, got[:, 0], got[:, 1]).reshape(group * passages, LANES)
            rows = slice(c * group * passages, (c + 1) * group * passages)
            pooled[rows, lanes] = (got + part_ref[rows, lanes]).astype(jnp.bfloat16)
        return carry

    lax.fori_loop(0, PAIRS, body, 0)
    mixed = jnp.dot(pooled[...], wo_ref[...], preferred_element_type=jnp.float32)
    mixed = (mixed.reshape(queries, passages, width) + resid_ref[...].astype(jnp.float32)[None]).reshape(
        queries * passages, width
    )
    mean = jnp.mean(mixed, axis=-1, keepdims=True)
    centered = mixed - mean
    var = jnp.mean(centered * centered, axis=-1, keepdims=True)
    normed = (centered * lax.rsqrt(var + norm_eps) * gain_ref[...] + bias_ref[...]).astype(jnp.bfloat16)
    hidden = jnp.tanh(jnp.dot(normed, wd_ref[...], preferred_element_type=jnp.float32) + bd_ref[...])
    score = jnp.sum((hidden * out_w_ref[...]).reshape(queries, passages, width), axis=-1)
    table[pl.ds(pl.multiple_of(step * queries, queries), queries), :] = score

    @pl.when(step == pl.num_programs(0) - 1)
    def _():
        teacher_ref[...] = table[...].T


def split_dot(a, b):
    high = a.astype(jnp.bfloat16)
    low = (a - high.astype(jnp.float32)).astype(jnp.bfloat16)
    return jnp.dot(high, b, preferred_element_type=jnp.float32) + jnp.dot(low, b, preferred_element_type=jnp.float32)


def loss_kernel(teacher_ref, student_ref, count_ref, slot_ref, sp_ref, sq_ref, index_ref, score_ref, loss_ref, gq_ref, gp_ref, held, rows_held):
    teacher, student, count = teacher_ref[...], student_ref[...], count_ref[...]
    total, queries = teacher.shape
    slots = slot_ref.shape[1]
    passages = gp_ref.shape[0]
    index = index_ref[0]
    live = count > 0.0

    def log_probs(scores):
        top = jnp.max(jnp.where(live, scores, -1e30), axis=0, keepdims=True)
        scaled = jnp.where(live, count * jnp.exp(jnp.where(live, scores - top, 0.0)), 0.0)
        return scores - top - jnp.log(jnp.sum(scaled, axis=0, keepdims=True))

    log_t, log_s = log_probs(teacher), log_probs(student)
    prob_t = jnp.where(live, count * jnp.exp(jnp.where(live, log_t, 0.0)), 0.0)
    prob_s = jnp.where(live, count * jnp.exp(jnp.where(live, log_s, 0.0)), 0.0)
    loss = jnp.sum(jnp.where(live, prob_t * (log_t - log_s), 0.0), axis=0, keepdims=True)
    mine = iota((1, queries), 1) == index
    loss_ref[...] = jnp.sum(jnp.where(mine, loss, 0.0), axis=1, keepdims=True)
    own_teacher = jnp.sum(jnp.where(mine, teacher, 0.0), axis=1, keepdims=True)
    hit = iota((total, slots), 0) == slot_ref[...]
    score_ref[...] = jnp.sum(jnp.where(hit, own_teacher, 0.0), axis=0, keepdims=True)
    grad = (prob_s - prob_t) * student_scale
    held[...] = grad
    own = held[pl.ds(pl.multiple_of(index * passages, passages), passages), :]
    gp_ref[...] = split_dot(own, sq_ref[...])
    rows_held[...] = grad.T
    row = rows_held[pl.ds(index, 1), :]
    gq_ref[...] = split_dot(jnp.broadcast_to(row, (8, total)), sp_ref[...])[:1]


def call(kernel, **kw):
    return pl.pallas_call(kernel, compiler_params=pltpu.CompilerParams(vmem_limit_bytes=VMEM_LIMIT), **kw)


def local(n_pb, n_pa, query_kv, student_query, block_holder, cand_local, counts, passage_qkv, passage_resid, student_passage, w_o, ln_gain, ln_bias, w_dense, b_dense, w_out):
    f32, bf16 = jnp.float32, jnp.bfloat16
    axes = ("pb", "pa")
    column = lax.axis_index("pa")
    index = lax.axis_index("pb") * n_pa + column
    nq = n_pb * n_pa
    passages, _, length, width = passage_qkv.shape
    keys = query_kv.shape[2]
    rows = passages * length
    total = nq * passages
    blocks, slot_len = cand_local.shape[1:]
    slots = blocks * slot_len

    own_cand = lax.dynamic_slice_in_dim(cand_local, column, 1, 0)[0].astype(jnp.int32)
    own_holder = lax.dynamic_slice_in_dim(block_holder, column, 1, 0)[0]
    own_count = lax.dynamic_slice_in_dim(counts, column, 1, 0)
    own_id = ((own_cand // passages) * n_pa + own_holder) * passages + own_cand % passages
    own_id = own_id.reshape(1, slots)
    own_id = jnp.where(jnp.arange(slots, dtype=jnp.int32)[None, :] < own_count[:, None], own_id, -1)

    numbers = jnp.concatenate([own_cand.reshape(-1), own_holder.reshape(-1), own_count]).astype(bf16)
    numbers = jnp.pad(numbers, (0, width - numbers.shape[0]))[None]
    extra = jnp.concatenate([student_passage, student_query, numbers, jnp.zeros((16 - passages - 2, width), bf16)], axis=0)
    first = jnp.concatenate([query_kv[:, 0], extra[None]], axis=1)
    got = lax.all_gather(first, axes, axis=0, tiled=True)
    value = lax.all_gather(query_kv[:, 1], axes, axis=0, tiled=True)

    self_out, self_lse = call(
        self_kernel,
        out_shape=(jax.ShapeDtypeStruct((rows, width), bf16), jax.ShapeDtypeStruct((PAIRS, 2, rows), f32)),
    )(passage_qkv)

    chunk = 8
    kwt, part = call(
        cross_kernel,
        grid=(nq // chunk,),
        in_specs=[
            pl.BlockSpec((chunk, keys, width), lambda i: (i, 0, 0)),
            pl.BlockSpec((passages, 1, length, width), lambda i: (0, 0, 0, 0)),
            pl.BlockSpec((rows, width), lambda i: (0, 0)),
            pl.BlockSpec((PAIRS, 2, rows), lambda i: (0, 0, 0)),
        ],
        out_specs=(
            pl.BlockSpec((PAIRS, 2 * passages, chunk * keys), lambda i: (0, 0, i)),
            pl.BlockSpec((chunk * passages, width), lambda i: (i, 0)),
        ),
        out_shape=(
            jax.ShapeDtypeStruct((PAIRS, 2 * passages, nq * keys), bf16),
            jax.ShapeDtypeStruct((total, width), f32),
        ),
    )(got, passage_qkv, self_out, self_lse)

    sp = got[:, keys : keys + passages].reshape(total, width)
    sq = got[:, keys + passages]
    ints = got[:, keys + passages + 1, : slots + blocks + 1].astype(jnp.int32)
    cand = ints[:, :slots]
    holder = jnp.repeat(ints[:, slots : slots + blocks], slot_len, axis=1)
    ids = ((cand // passages) * n_pa + holder) * passages + cand % passages
    ids = jnp.where(jnp.arange(slots, dtype=jnp.int32)[None, :] < ints[:, slots + blocks :], ids, -1)
    count = jnp.sum((ids[None, :, :] == jnp.arange(total, dtype=jnp.int32)[:, None, None]).astype(f32), axis=2)
    student = student_scale * lax.dot_general(sp, sq, NT, preferred_element_type=f32)

    step = 16
    whole = lambda *shape: pl.BlockSpec(shape, lambda i: (0,) * len(shape))
    teacher = call(
        head_kernel,
        grid=(nq // step,),
        in_specs=[
            pl.BlockSpec((step, keys, width), lambda i: (i, 0, 0)),
            pl.BlockSpec((PAIRS, 2 * passages, step * keys), lambda i: (0, 0, i)),
            pl.BlockSpec((step * passages, width), lambda i: (i, 0)),
            whole(passages, width),
            whole(width, width),
            whole(1, width),
            whole(1, width),
            whole(width, width),
            whole(1, width),
            whole(1, width),
        ],
        out_specs=whole(passages, nq),
        out_shape=jax.ShapeDtypeStruct((passages, nq), f32),
        scratch_shapes=[pltpu.VMEM((step * passages, width), bf16), pltpu.VMEM((nq, passages), f32)],
    )(value, kwt, part, passage_resid, w_o, ln_gain[None], ln_bias[None], w_dense, b_dense[None], w_out[None])

    teacher_all = lax.all_gather(teacher, axes, axis=0, tiled=True)
    vmem = pl.BlockSpec(memory_space=pltpu.VMEM)
    scores, loss, grad_query, grad_passage = call(
        loss_kernel,
        in_specs=[vmem] * 6 + [pl.BlockSpec(memory_space=pltpu.SMEM)],
        out_shape=(
            jax.ShapeDtypeStruct((1, slots), f32),
            jax.ShapeDtypeStruct((1, 1), f32),
            jax.ShapeDtypeStruct((1, width), f32),
            jax.ShapeDtypeStruct((passages, width), f32),
        ),
        scratch_shapes=[pltpu.VMEM((total, nq), f32), pltpu.VMEM((nq, total), f32)],
    )(teacher_all, student, count, own_id, sp, sq, index.reshape(1).astype(jnp.int32))
    return scores, loss.reshape(1), grad_query, grad_passage


def solution(mesh):
    placed = (
        P(("pb", "pa"), None, None, None),
        P(("pb", "pa"), None),
        P("pb", None, None),
        P("pb", None, None),
        P("pb"),
        P(("pa", "pb"), None, None, None),
        P(("pa", "pb"), None),
        P(("pa", "pb"), None),
        P(),
        P(),
        P(),
        P(),
        P(),
        P(),
    )
    return jax.shard_map(
        functools.partial(local, mesh.shape["pb"], mesh.shape["pa"]),
        mesh=mesh,
        in_specs=placed,
        out_specs=(P(("pb", "pa"), None), P(("pb", "pa")), P(("pb", "pa"), None), P(("pa", "pb"), None)),
        check_vma=False,
    )
```

time: 354 us -> 231 us (0.65)
  local copies, waits for them, and re-layouts: 135 us -> 7.59 us
  waiting for transfers between devices: 20.6 us -> 78.7 us
  Pallas kernels: 0 us -> 50.2 us
  matrix products: 45.9 us -> 1.96 us
  other arithmetic: 38.9 us -> 4.87 us
  blocking collectives: 87.8 us -> 72.4 us
  loops' own time: 8.72 us -> 0 us
    all_gather x2, waiting for transfers between devices: 9.22 us -> 78 us  [the longest x1 50.1 us: local(): got = lax.all_gather(first, axes, axis=0, tiled=True)]
    reshape x20 -> x2, local copies, waits for them, and re-layouts: 62.9 us -> 1.97 us  [the longest x1 1.88 us: local(): sp = got[:, keys:keys + passages].reshape(total, width)]
    pallas_call x0 -> x4, Pallas kernels: none -> 50.2 us  [the longest x1 29.2 us: local(): call(cross_kernel, grid=(nq // chunk,), in_specs=[pl.BlockSpec((chunk, ke...]
    dot_general x33 -> x1, matrix products: 45.9 us -> 1.96 us  [local(): lax.dot_general(sp, sq, NT, preferred_element_type=f32)]
    gather x24 -> x0, local copies, waits for them, and re-layouts: 39.6 us -> none  [the longest x4 12 us: one_slot(): pool_out[pool_rows]]
    reduce_sum x16 -> x1, other arithmetic: 26.4 us -> 0.47 us  [local(): jnp.sum((ids[None, :, :] == jnp.arange(total, dtype=jnp.int32)[:, None, N...]
    unnamed x1 -> x0, blocking collectives: 15.5 us -> none
    all_gather x5 -> x1, blocking collectives: 60.6 us -> 72.4 us  [local(): teacher_all = lax.all_gather(teacher, axes, axis=0, tiled=True)]
  transfers between devices with their start and end apart: 3 -> 2, of which waited for: 2 -> 2; matrix products, arithmetic and copies ran while one was open for 4% -> 1% of each run, Pallas kernels for 0% -> 17%
where the time goes in v1:
time: 231 us
  waiting for transfers between devices  78.7 us (34%)
  blocking collectives  72.4 us (31%)
  Pallas kernels  50.2 us (22%)
  between operations  14.8 us (6%)
  local copies, waits for them, and re-layouts  7.59 us (3%)
  other arithmetic  4.87 us (2%)
    all_gather x1, blocking collectives, local(): teacher_all = lax.all_gather(teacher, axes, axis=0, tiled=True)  72.4 us
    all_gather x1, waiting for transfers between devices, local(): got = lax.all_gather(first, axes, axis=0, tiled=True)  50.1 us
    pallas_call x1, Pallas kernels, local(): call(cross_kernel, grid=(nq // chunk,), in_specs=[pl.BlockSpec((chunk, ke...  29.2 us
    all_gather x1, waiting for transfers between devices, local(): value = lax.all_gather(query_kv[:, 1], axes, axis=0, tiled=True)  28 us
    pallas_call x1, Pallas kernels, local(): call(self_kernel, out_shape=(jax.ShapeDtypeStruct((rows, width), bf16), j...  9.65 us
    pallas_call x1, Pallas kernels, local(): call(head_kernel, grid=(nq // step,), in_specs=[pl.BlockSpec((step, keys,...  8.97 us
  transfers between devices with their start and end apart: 2, of which 2 were waited for; matrix products, arithmetic and copies ran while one was open for 1% of the time, Pallas kernels for 17%

profile of v1, /device:TPU:0, one launch (start us, length us, event | category | flops | bytes accessed | tf_op | source)
XLA Modules:
  0.0 230.6 jit_solution(16270370565883311692)
XLA Ops:
  7.2 0.0 copy-start
  7.2 0.0 all-gather.4.cloned.1.call-start
  7.2 0.7 fusion.15
  7.9 0.1 reshape_squeeze.7
  8.0 0.0 copy-done
  8.0 0.2 dynamic-slice_reduce_fusion
  8.2 1.2 dynamic_slice.11
  10.1 0.1 fusion.13
  10.2 1.5 slice_bitcast_fusion.1
  11.7 0.1 pad.10.clone
  11.8 0.8 maximum_bitcast_fusion
  12.6 0.6 pad_maximum_fusion
  13.2 0.0 all-gather.4.cloned.1.call-update
  13.3 0.0 all-gather.6.cloned.1.call-start
  13.3 0.7 all-gather.6.cloned.1.call-update
  14.0 9.6 %shard_map.165 = (bf16[256,1024]{1,0:T(8,128)(2,1)}, f32[8,2,256]{2,1,0:T(2,128)}) custom-call(bf16[8,3,32,1024]{3,2,1,0:T(8,128)(2,1)} %q_ref.1), custom_call_target="tpu_custom_call" | custom-call | tf_op jit(solution)/shard_map/pallas_call | solution.py:210
  23.7 0.1 squeeze.17
  23.7 0.1 add.79
  23.8 0.1 add.80
  23.9 1.2 compare_select_fusion.slot_ref
  25.1 50.1 %all-gather.4.cloned.1.call-done.k_ref = bf16[32,48,1024]{2,1,0:T(8,128)(2,1)} async-done(((bf16[1,48,1024]{2,1,0:T(8,128)(2,1)}), bf16[32,48,1024]{2,1,0:T(8,128)(2,1)}) %all-gather.4.cloned.1.call-update) | async-done | bytes 3145744 | tf_op jit(solution)/shard_map/all_gather | solution.py:207
  75.2 0.9 slice_convert_fusion
  76.1 0.1 slice.37
  76.1 29.2 %shard_map.166 = (bf16[8,16,1024]{2,1,0:T(8,128)(2,1)}, f32[256,1024]{1,0:T(8,128)}) custom-call(bf16[32,48,1024]{2,1,0:T(8,128)(2,1)} %all-gather.4.cloned.1.call-done.k_ref, bf16[8,3,32,1024]{3,2,1,0:T(8,128)(2,1)} %q_ref.1, bf16[256,1024]{1,0:T(8,128)(2,1)} %get-tuple-element.12.so_ref, f32[8,2,256]{2,1,0:T(2,128)} %get-tuple-element.13.lse_ref), custom_call_target="tpu_custom_call" | custom-call | tf_op jit(solution)/shard_map/pallas_call | solution.py:216
  105.4 0.2 slice_reduce_fusion
  105.5 28.0 %all-gather.6.cloned.1.call-done = bf16[32,1,32,1024]{3,2,1,0:T(8,128)(2,1)} async-done(((bf16[1,1,32,1024]{3,2,1,0:T(8,128)(2,1)}), bf16[32,1,32,1024]{3,2,1,0:T(8,128)(2,1)}) %all-gather.6.cloned.1.call-update) | async-done | bytes 2097168 | tf_op jit(solution)/shard_map/all_gather | solution.py:208
  133.5 9.0 %shard_map.167 = f32[8,32]{1,0:T(8,128)} custom-call(bf16[32,32,1024]{2,1,0:T(8,128)(2,1)} %bitcast.20, bf16[8,16,1024]{2,1,0:T(8,128)(2,1)} %get-tuple-element.14.kwt_ref, f32[256,1024]{1,0:T(8,128)} %get-tuple-element.15.part_ref, bf16[8,1024]{1,0:T(8,128)(2,1)} %resid_ref.1, bf16[1024,1024]{1,0:T(8,128)(2,1)} %wo_ref.1, f32[1,1024]{1,0:T(1,128)} %bitcast.26, ...), custom_call_target="tpu_custom_call" | custom-call | tf_op jit(solution)/shard_map/pallas_call | solution.py:247
  142.5 72.4 %all_gather.11.teacher_ref = f32[256,32]{1,0:T(8,128)} all-gather(f32[8,32]{1,0:T(8,128)} %shard_map.167), channel_id=1, replica_groups=mesh['pb'=8,'pa'=4] {'pb','pa'}, dimensions={0}, use_global_device_ids=true | all-gather | bytes 33792 | tf_op jit(solution)/shard_map/all_gather | solution.py:267
  214.8 0.1 broadcast_in_dim.40
  214.9 0.1 reshape.158
  215.0 0.1 fusion.4
  215.1 0.5 convert_reduce_fusion
  215.6 0.8 copy.35.count_ref
  216.3 1.1 slice.33
  217.5 0.0 copy-start.1
  217.5 1.9 slice_bitcast_fusion.sp_ref
  219.4 2.0 convolution_multiply_fusion.student_ref
  221.4 0.0 copy-done.1
  221.4 2.4 %shard_map.168 = (f32[1,64]{1,0:T(1,128)}, f32[1,1]{1,0:T(1,128)}, f32[1,1024]{1,0:T(1,128)}, f32[8,1024]{1,0:T(8,128)}) custom-call(f32[256,32]{1,0:T(8,128)} %all_gather.11.teacher_ref, f32[256,32]{1,0:T(8,128)} %convolution_multiply_fusion.student_ref, f32[256,32]{1,0:T(8,128)} %copy.35.count_ref, s32[1,64]{1,0:T(1,128)} %compare_select_fusion.slot_ref, ...), custom_call_target="tpu_custom_call" | custom-call | tf_op jit(solution)/shard_map/pallas_call | solution.py:269
  (4 shorter events, 0.0 us)
Async XLA Ops:
  7.2 0.8 copy-start
  7.2 68.0 %all-gather.4.cloned.1.call-start = ((), (), s32[]{:S(2)}) async-start(), calls=%async_computation | async-start | bytes 3244032 | tf_op jit(solution)/shard_map/all_gather | solution.py:207
  13.3 120.2 %all-gather.6.cloned.1.call-start = ((), (), s32[]{:S(2)}) async-start(), calls=%async_computation.1 | async-start | bytes 2162688 | tf_op jit(solution)/shard_map/all_gather | solution.py:208
  217.5 3.9 %copy-start.1 = (bf16[32,1,1024]{2,0,1:T(8,128)(2,1)}, bf16[32,1,1024]{2,0,1:T(8,128)(2,1)S(1)}, u32[]{:S(2)}) copy-start(bf16[32,1,1024]{2,0,1:T(8,128)(2,1)S(1)} %copy.39) | copy-start | bytes 196612
Sparse Core Ops, SparseCore 0:
  13.4 61.7 all-gather.3
  78.1 55.3 all-gather.5

commit v2 on v1

v2 whole, which is shorter than its diff:
```python
import functools

import jax
import jax.numpy as jnp
from jax import lax
from jax.experimental import pallas as pl
from jax.experimental.pallas import tpu as pltpu
from jax.sharding import PartitionSpec as P

HEADS = 16
HEAD_DIM = 64
PAIRS = HEADS // 2
BLOCK = 32
BLOCKS = 2
LANES = 128
student_scale = 0.125
norm_eps = 1e-05
VMEM_LIMIT = 56 * 1024 * 1024
NT = (((1,), (1,)), ((), ()))


def iota(shape, axis):
    return lax.broadcasted_iota(jnp.int32, shape, axis)


def pair_masks(rows):
    low = iota((rows, LANES), 1) < HEAD_DIM
    return low, jnp.logical_not(low)


def attend_pair(qkv_ref, out_ref, lse_ref, k):
    passages, _, length, _ = qkv_ref.shape
    rows = passages * length
    masks = pair_masks(rows)
    same = iota((rows, rows), 0) // length == iota((rows, rows), 1) // length
    lanes = pl.ds(pl.multiple_of(k * LANES, LANES), LANES)
    q = qkv_ref[:, 0, :, lanes].reshape(rows, LANES)
    key = qkv_ref[:, 1, :, lanes].reshape(rows, LANES)
    value = qkv_ref[:, 2, :, lanes].reshape(rows, LANES)
    outs, lses = [], []
    for mask in masks:
        q_head = jnp.where(mask, q.astype(jnp.float32) * 0.125, 0.0).astype(jnp.bfloat16)
        scores = lax.dot_general(key, q_head, NT, preferred_element_type=jnp.float32)
        scores = jnp.where(same, scores, -1e30)
        top = jnp.max(scores, axis=0, keepdims=True)
        scaled = jnp.exp(scores - top)
        total = jnp.sum(scaled, axis=0, keepdims=True)
        lses.append(top + jnp.log(total))
        probs = (scaled * (1.0 / total)).T.astype(jnp.bfloat16)
        outs.append(jnp.dot(probs, value, preferred_element_type=jnp.float32))
    out_ref[:, lanes] = jnp.where(masks[0], outs[0], outs[1]).astype(jnp.bfloat16)
    lse_ref[k] = jnp.concatenate(lses, axis=0)


def gather_kernel(n_pb, n_pa, first_ref, value_ref, qkv_ref, got_ref, vals_ref, out_ref, lse_ref, send, recv, here):
    me_b, me_a = lax.axis_index("pb"), lax.axis_index("pa")
    core = me_b % 2
    spot = me_b // 2
    sx, sy = spot % 2, spot // 2
    beside = (sy * 2 + 1 - sx) * 2 + core
    across = ((1 - sy) * 2 + sx) * 2 + core
    corner = ((1 - sy) * 2 + 1 - sx) * 2 + core
    other = spot * 2 + 1 - core
    bufs = (got_ref, vals_ref)

    def copy(kind, piece, slot, owner_b, to_b, to_a):
        owner_a = (me_a + n_pa - slot) % n_pa
        ref = bufs[piece].at[owner_b * n_pa + owner_a]
        return pltpu.make_async_remote_copy(
            src_ref=ref,
            dst_ref=ref,
            send_sem=send.at[kind * 2 + piece, slot],
            recv_sem=recv.at[kind * 2 + piece, slot],
            device_id=(to_b, to_a),
            device_id_type=pl.DeviceIdType.MESH,
        )

    def along(piece, step):
        ref = bufs[piece].at[me_b * n_pa + me_a]
        return pltpu.make_async_remote_copy(
            src_ref=ref,
            dst_ref=ref,
            send_sem=send.at[piece, step],
            recv_sem=recv.at[piece, step],
            device_id=(me_b, (me_a + step) % n_pa),
            device_id_type=pl.DeviceIdType.MESH,
        )

    def arrived(kind, piece, slot, owner_b):
        copy(kind, piece, slot, owner_b, other, me_a).wait_recv()

    barrier = pltpu.get_barrier_semaphore()
    for peer in (beside, across, other):
        pl.semaphore_signal(barrier, inc=1, device_id=(peer, me_a), device_id_type=pl.DeviceIdType.MESH)

    def greet(step, carry):
        pl.semaphore_signal(
            barrier, inc=1, device_id=(me_b, (me_a + step) % n_pa), device_id_type=pl.DeviceIdType.MESH
        )
        return carry

    lax.fori_loop(1, n_pa, greet, 0)
    mine = me_b * n_pa + me_a
    own_copies = [
        pltpu.make_async_copy(first_ref.at[0], got_ref.at[mine], here.at[0]),
        pltpu.make_async_copy(value_ref.at[0], vals_ref.at[mine], here.at[1]),
    ]
    for one in own_copies:
        one.start()
    for one in own_copies:
        one.wait()
    pl.semaphore_wait(barrier, n_pa + 2)

    def column(step, carry):
        along(0, step).start()
        along(1, step).start()
        return carry

    def plane(slot, carry):
        @pl.when(slot > 0)
        def _():
            arrived(0, 0, slot, me_b)
            arrived(0, 1, slot, me_b)

        for piece in range(2):
            copy(1, piece, slot, me_b, beside, me_a).start()
            copy(2, piece, slot, me_b, across, me_a).start()
            copy(4, piece, slot, me_b, other, me_a).start()

        @pl.when(slot < 4)
        def _():
            for half in range(PAIRS // 4):
                attend_pair(qkv_ref, out_ref, lse_ref, slot * (PAIRS // 4) + half)

        return carry

    def forward(slot, carry):
        arrived(1, 0, slot, beside)
        copy(3, 0, slot, beside, across, me_a).start()
        copy(5, 0, slot, beside, other, me_a).start()
        arrived(2, 1, slot, across)
        copy(3, 1, slot, across, beside, me_a).start()
        copy(6, 1, slot, across, other, me_a).start()
        arrived(1, 1, slot, beside)
        copy(5, 1, slot, beside, other, me_a).start()
        arrived(2, 0, slot, across)
        copy(6, 0, slot, across, other, me_a).start()
        return carry

    def last(slot, carry):
        for piece in range(2):
            arrived(3, piece, slot, corner)
            copy(7, piece, slot, corner, other, me_a).start()
        return carry

    def finish(slot, carry):
        for piece in range(2):
            for kind, owner in ((4, me_b), (5, beside), (6, across), (7, corner)):
                far = owner + 1 - 2 * core
                arrived(kind, piece, slot, far)
                copy(kind, piece, slot, owner, other, me_a).wait_send()
            copy(1, piece, slot, me_b, beside, me_a).wait_send()
            copy(2, piece, slot, me_b, across, me_a).wait_send()
        copy(3, 0, slot, beside, across, me_a).wait_send()
        copy(3, 1, slot, across, beside, me_a).wait_send()

        @pl.when(slot > 0)
        def _():
            along(0, slot).wait_send()
            along(1, slot).wait_send()

        return carry

    lax.fori_loop(1, n_pa, column, 0)
    lax.fori_loop(0, n_pa, plane, 0)
    lax.fori_loop(0, n_pa, forward, 0)
    lax.fori_loop(0, n_pa, last, 0)
    lax.fori_loop(0, n_pa, finish, 0)


def share_kernel(n_pb, n_pa, own_ref, all_ref, send, recv, here):
    me_b, me_a = lax.axis_index("pb"), lax.axis_index("pa")
    count = n_pb * n_pa
    me = me_b * n_pa + me_a

    def place(step):
        to = (me + step) % count
        return (to // n_pa, to % n_pa)

    def copy(step):
        return pltpu.make_async_remote_copy(
            src_ref=own_ref,
            dst_ref=all_ref.at[me],
            send_sem=send.at[step],
            recv_sem=recv.at[step],
            device_id=place(step),
            device_id_type=pl.DeviceIdType.MESH,
        )

    def came(step):
        source = (me + count - step) % count
        return pltpu.make_async_remote_copy(
            src_ref=own_ref,
            dst_ref=all_ref.at[source],
            send_sem=send.at[step],
            recv_sem=recv.at[step],
            device_id=place(step),
            device_id_type=pl.DeviceIdType.MESH,
        )

    barrier = pltpu.get_barrier_semaphore()

    def greet(step, carry):
        pl.semaphore_signal(barrier, inc=1, device_id=place(step), device_id_type=pl.DeviceIdType.MESH)
        return carry

    def start(step, carry):
        copy(step).start()
        return carry

    def finish(step, carry):
        came(step).wait_recv()
        copy(step).wait_send()
        return carry

    lax.fori_loop(1, count, greet, 0)
    own_copy = pltpu.make_async_copy(own_ref, all_ref.at[me], here.at[0])
    own_copy.start()
    pl.semaphore_wait(barrier, count - 1)
    lax.fori_loop(1, count, start, 0)
    own_copy.wait()
    lax.fori_loop(1, count, finish, 0)


def list_kernel(n_pa, index_ref, extra_ref, sp_ref, sq_ref, student_ref, count_ref, order_ref, held):
    queries, _, width = extra_ref.shape
    total = sp_ref.shape[0]
    passages = total // queries
    extra = extra_ref[...].astype(jnp.float32)
    sp = extra[:, :passages].reshape(total, width).astype(jnp.bfloat16)
    rest = extra[:, passages:]
    sq = rest[:, 0].astype(jnp.bfloat16)
    sp_ref[...] = sp
    sq_ref[...] = sq
    student_ref[...] = student_scale * lax.dot_general(sp, sq, NT, preferred_element_type=jnp.float32)
    ids = rest[:, 1, :LANES].T
    slots = BLOCK * BLOCKS
    row = iota((total, queries), 0).astype(jnp.float32)
    number = jnp.floor(row / passages)
    part = row - number * passages
    group = jnp.floor(number / n_pa)
    holder_of = number - group * n_pa
    local_of = group * passages + part
    real = ids[slots + BLOCKS : slots + BLOCKS + 1]
    count = jnp.zeros((total, queries), jnp.float32)
    for b in range(BLOCKS):
        tally = jnp.zeros((total, queries), jnp.float32)
        for c in range(b * BLOCK, (b + 1) * BLOCK):
            name = jnp.where(real > c, ids[c : c + 1], -1.0)
            tally = tally + (local_of == name).astype(jnp.float32)
        count = count + jnp.where(holder_of == ids[slots + b : slots + b + 1], tally, 0.0)
    count_ref[...] = count
    held[...] = count
    own = held[pl.ds(pl.multiple_of(index_ref[0] * passages, passages), passages), :]
    need = (jnp.max(own, axis=0, keepdims=True) > 0.0).astype(jnp.float32)
    lane, col = iota((queries, queries), 0), iota((queries, queries), 1)
    need_col = jnp.sum(jnp.where(lane == col, need, 0.0), axis=1, keepdims=True)
    before = jnp.sum(jnp.where(lane < col, need_col, 0.0), axis=0, keepdims=True)
    needed = jnp.sum(need, axis=1, keepdims=True)
    spot = iota((1, queries), 1).astype(jnp.float32)
    place = jnp.where(need > 0.0, before, needed + spot - before)
    order = jnp.sum(jnp.where(place == lane.astype(jnp.float32), col.astype(jnp.float32), 0.0), axis=1, keepdims=True)
    order = jnp.sum(jnp.where(lane == col, order, 0.0), axis=0, keepdims=True)
    order_ref[...] = jnp.concatenate([order, jnp.broadcast_to(needed, (1, queries))], axis=0).astype(jnp.int32)


def cross_kernel(queries, order_ref, k_ref, q_ref, so_ref, lse_ref, kwt_ref, part_ref):
    step = pl.program_id(0)
    keys = k_ref.shape[1]
    passages, _, length, _ = q_ref.shape
    rows = passages * length
    masks = pair_masks(rows)
    out_low = iota((queries * passages, LANES), 1) < HEAD_DIM
    own = (iota((passages, rows), 1) // length == iota((passages, rows), 0)).astype(jnp.float32)
    spots = [
        jnp.where(iota((rows, LANES), 1) == iota((rows, LANES), 0) // length + h * passages, 1.0 / length, 0.0).astype(
            jnp.bfloat16
        )
        for h in range(2)
    ]

    def body(k, carry):
        lanes = pl.ds(pl.multiple_of(k * LANES, LANES), LANES)
        q = q_ref[:, 0, :, lanes].reshape(rows, LANES)
        key = jnp.concatenate([k_ref[order_ref[0, step * queries + i], :, lanes] for i in range(queries)], axis=0)
        so = so_ref[:, lanes]
        lse = lse_ref[k]
        weights, parts = None, []
        for h in range(2):
            q_head = jnp.where(masks[h], q.astype(jnp.float32) * 0.125, 0.0).astype(jnp.bfloat16)
            scores = lax.dot_general(key, q_head, NT, preferred_element_type=jnp.float32)
            scores = scores.reshape(queries, keys, rows)
            self_lse = lse[h : h + 1]
            top = jnp.maximum(jnp.max(scores, axis=1), self_lse)
            scaled = jnp.exp(scores - top[:, None, :])
            self_term = jnp.exp(self_lse - top)
            inverse = 1.0 / (jnp.sum(scaled, axis=1) + self_term)
            spread = (scaled * inverse[:, None, :]).reshape(queries * keys, rows).astype(jnp.bfloat16)
            weight = jnp.dot(spread, spots[h], preferred_element_type=jnp.float32)
            weights = weight if weights is None else weights + weight
            token = self_term * inverse * (1.0 / length)
            token = (token[:, None, :] * own[None]).reshape(queries * passages, rows).astype(jnp.bfloat16)
            parts.append(jnp.dot(token, so, preferred_element_type=jnp.float32))
        part_ref[:, lanes] = jnp.where(out_low, parts[0], parts[1])
        kwt_ref[k] = weights.T[: 2 * passages].astype(jnp.bfloat16)
        return carry

    @pl.when(step * queries < order_ref[1, 0])
    def _():
        lax.fori_loop(0, PAIRS, body, 0)


def head_kernel(queries, order_ref, v_ref, kwt_ref, part_ref, resid_ref, wo_ref, gain_ref, bias_ref, wd_ref, bd_ref, out_w_ref, teacher_ref, pooled, table):
    step = pl.program_id(0)
    _, keys, width = v_ref.shape
    passages = resid_ref.shape[0]
    group = 8
    cols = group * keys
    span = 2 * passages
    own = (iota((group, span, cols), 2) // keys == iota((group, span, cols), 0)).astype(jnp.float32)
    low = iota((group, passages, LANES), 2) < HEAD_DIM

    def body(k, carry):
        lanes = pl.ds(pl.multiple_of(k * LANES, LANES), LANES)
        for c in range(queries // group):
            weight = kwt_ref[k, :, c * cols : (c + 1) * cols].astype(jnp.float32)
            weight = (weight[None] * own).reshape(group * span, cols).astype(jnp.bfloat16)
            value = jnp.concatenate(
                [v_ref[order_ref[0, step * queries + c * group + i], :, lanes] for i in range(group)], axis=0
            )
            got = jnp.dot(weight, value, preferred_element_type=jnp.float32)
            got = got.reshape(group, 2, passages, LANES)
            got = jnp.where(low, got[:, 0], got[:, 1]).reshape(group * passages, LANES)
            rows = slice(c * group * passages, (c + 1) * group * passages)
            pooled[rows, lanes] = (got + part_ref[rows, lanes]).astype(jnp.bfloat16)
        return carry

    @pl.when(step == 0)
    def _():
        table[...] = jnp.zeros_like(table)

    @pl.when(step * queries < order_ref[1, 0])
    def _():
        lax.fori_loop(0, PAIRS, body, 0)
        mixed = jnp.dot(pooled[...], wo_ref[...], preferred_element_type=jnp.float32)
        mixed = (mixed.reshape(queries, passages, width) + resid_ref[...].astype(jnp.float32)[None]).reshape(
            queries * passages, width
        )
        mean = jnp.mean(mixed, axis=-1, keepdims=True)
        centered = mixed - mean
        var = jnp.mean(centered * centered, axis=-1, keepdims=True)
        normed = (centered * lax.rsqrt(var + norm_eps) * gain_ref[...] + bias_ref[...]).astype(jnp.bfloat16)
        hidden = jnp.tanh(jnp.dot(normed, wd_ref[...], preferred_element_type=jnp.float32) + bd_ref[...])
        score = jnp.sum((hidden * out_w_ref[...]).reshape(queries, passages, width), axis=-1)
        for i in range(queries):
            table[pl.ds(order_ref[0, step * queries + i], 1), :] = score[i : i + 1]

    @pl.when(step == pl.num_programs(0) - 1)
    def _():
        teacher_ref[...] = table[...].T


def split_dot(a, b):
    high = a.astype(jnp.bfloat16)
    low = (a - high.astype(jnp.float32)).astype(jnp.bfloat16)
    return jnp.dot(high, b, preferred_element_type=jnp.float32) + jnp.dot(low, b, preferred_element_type=jnp.float32)


def loss_kernel(teacher_ref, student_ref, count_ref, slot_ref, sp_ref, sq_ref, index_ref, score_ref, loss_ref, gq_ref, gp_ref, held, rows_held):
    teacher, student, count = teacher_ref[...], student_ref[...], count_ref[...]
    total, queries = teacher.shape
    slots = slot_ref.shape[1]
    passages = gp_ref.shape[0]
    index = index_ref[0]
    live = count > 0.0

    def log_probs(scores):
        top = jnp.max(jnp.where(live, scores, -1e30), axis=0, keepdims=True)
        scaled = jnp.where(live, count * jnp.exp(jnp.where(live, scores - top, 0.0)), 0.0)
        return scores - top - jnp.log(jnp.sum(scaled, axis=0, keepdims=True))

    log_t, log_s = log_probs(teacher), log_probs(student)
    prob_t = jnp.where(live, count * jnp.exp(jnp.where(live, log_t, 0.0)), 0.0)
    prob_s = jnp.where(live, count * jnp.exp(jnp.where(live, log_s, 0.0)), 0.0)
    loss = jnp.sum(jnp.where(live, prob_t * (log_t - log_s), 0.0), axis=0, keepdims=True)
    mine = iota((1, queries), 1) == index
    loss_ref[...] = jnp.sum(jnp.where(mine, loss, 0.0), axis=1, keepdims=True)
    own_teacher = jnp.sum(jnp.where(mine, teacher, 0.0), axis=1, keepdims=True)
    hit = iota((total, slots), 0) == slot_ref[...]
    score_ref[...] = jnp.sum(jnp.where(hit, own_teacher, 0.0), axis=0, keepdims=True)
    grad = (prob_s - prob_t) * student_scale
    held[...] = grad
    own = held[pl.ds(pl.multiple_of(index * passages, passages), passages), :]
    gp_ref[...] = split_dot(own, sq_ref[...])
    rows_held[...] = grad.T
    row = rows_held[pl.ds(index, 1), :]
    gq_ref[...] = split_dot(jnp.broadcast_to(row, (8, total)), sp_ref[...])[:1]


def call(kernel, **kw):
    return pl.pallas_call(kernel, compiler_params=pltpu.CompilerParams(vmem_limit_bytes=VMEM_LIMIT), **kw)


def remote_call(kernel, number, **kw):
    params = pltpu.CompilerParams(vmem_limit_bytes=VMEM_LIMIT, collective_id=number, has_side_effects=True)
    return pl.pallas_call(kernel, compiler_params=params, **kw)


def local(n_pb, n_pa, query_kv, student_query, block_holder, cand_local, counts, passage_qkv, passage_resid, student_passage, w_o, ln_gain, ln_bias, w_dense, b_dense, w_out):
    f32, bf16 = jnp.float32, jnp.bfloat16
    axes = ("pb", "pa")
    column = lax.axis_index("pa")
    index = lax.axis_index("pb") * n_pa + column
    nq = n_pb * n_pa
    passages, _, length, width = passage_qkv.shape
    keys = query_kv.shape[2]
    rows = passages * length
    total = nq * passages
    blocks, slot_len = cand_local.shape[1:]
    slots = blocks * slot_len

    own_cand = lax.dynamic_slice_in_dim(cand_local, column, 1, 0)[0].astype(jnp.int32)
    own_holder = lax.dynamic_slice_in_dim(block_holder, column, 1, 0)[0]
    own_count = lax.dynamic_slice_in_dim(counts, column, 1, 0)
    own_id = ((own_cand // passages) * n_pa + own_holder) * passages + own_cand % passages
    own_id = own_id.reshape(1, slots)
    own_id = jnp.where(jnp.arange(slots, dtype=jnp.int32)[None, :] < own_count[:, None], own_id, -1)

    numbers = jnp.concatenate([own_cand.reshape(-1), own_holder.reshape(-1), own_count]).astype(bf16)
    numbers = jnp.pad(numbers, (0, width - numbers.shape[0]))[None]
    extra = jnp.concatenate([student_passage, student_query, numbers, jnp.zeros((16 - passages - 2, width), bf16)], axis=0)
    first = jnp.concatenate([query_kv[:, 0], extra[None]], axis=1)
    anywhere, vmem, smem = (pl.BlockSpec(memory_space=m) for m in (pl.ANY, pltpu.VMEM, pltpu.SMEM))
    got, value, self_out, self_lse = remote_call(
        functools.partial(gather_kernel, n_pb, n_pa),
        1,
        in_specs=[anywhere, anywhere, vmem],
        out_specs=(anywhere, anywhere, vmem, vmem),
        out_shape=(
            jax.ShapeDtypeStruct((nq,) + first.shape[1:], bf16),
            jax.ShapeDtypeStruct((nq, keys, width), bf16),
            jax.ShapeDtypeStruct((rows, width), bf16),
            jax.ShapeDtypeStruct((PAIRS, 2, rows), f32),
        ),
        scratch_shapes=[
            pltpu.SemaphoreType.DMA((16, n_pa)),
            pltpu.SemaphoreType.DMA((16, n_pa)),
            pltpu.SemaphoreType.DMA((2,)),
        ],
    )(first, query_kv[:, 1], passage_qkv)

    device = index.reshape(1).astype(jnp.int32)
    sp, sq, student, count, order = call(
        functools.partial(list_kernel, n_pa),
        grid=(1,),
        in_specs=[smem, pl.BlockSpec((nq, 16, width), lambda i: (0, keys // 16, 0))],
        out_specs=tuple(
            pl.BlockSpec(shape, lambda i: (0, 0)) for shape in ((total, width), (nq, width), (total, nq), (total, nq), (2, nq))
        ),
        out_shape=(
            jax.ShapeDtypeStruct((total, width), bf16),
            jax.ShapeDtypeStruct((nq, width), bf16),
            jax.ShapeDtypeStruct((total, nq), f32),
            jax.ShapeDtypeStruct((total, nq), f32),
            jax.ShapeDtypeStruct((2, nq), jnp.int32),
        ),
        scratch_shapes=[pltpu.VMEM((total, nq), f32)],
    )(device, got)

    whole = lambda *shape: pl.BlockSpec(shape, lambda i, o: (0,) * len(shape))
    chunk = 8
    kwt, part = call(
        functools.partial(cross_kernel, chunk),
        grid_spec=pltpu.PrefetchScalarGridSpec(
            num_scalar_prefetch=1,
            grid=(nq // chunk,),
            in_specs=[
                whole(nq, keys, width),
                whole(passages, 1, length, width),
                whole(rows, width),
                whole(PAIRS, 2, rows),
            ],
            out_specs=(
                pl.BlockSpec((PAIRS, 2 * passages, chunk * keys), lambda i, o: (0, 0, i)),
                pl.BlockSpec((chunk * passages, width), lambda i, o: (i, 0)),
            ),
        ),
        out_shape=(
            jax.ShapeDtypeStruct((PAIRS, 2 * passages, nq * keys), bf16),
            jax.ShapeDtypeStruct((total, width), f32),
        ),
    )(order, got, passage_qkv, self_out, self_lse)

    step = 16
    teacher = call(
        functools.partial(head_kernel, step),
        grid_spec=pltpu.PrefetchScalarGridSpec(
            num_scalar_prefetch=1,
            grid=(nq // step,),
            in_specs=[
                whole(nq, keys, width),
                pl.BlockSpec((PAIRS, 2 * passages, step * keys), lambda i, o: (0, 0, i)),
                pl.BlockSpec((step * passages, width), lambda i, o: (i, 0)),
                whole(passages, width),
                whole(width, width),
                whole(1, width),
                whole(1, width),
                whole(width, width),
                whole(1, width),
                whole(1, width),
            ],
            out_specs=whole(passages, nq),
            scratch_shapes=[pltpu.VMEM((step * passages, width), bf16), pltpu.VMEM((nq, passages), f32)],
        ),
        out_shape=jax.ShapeDtypeStruct((passages, nq), f32),
    )(order, value, kwt, part, passage_resid, w_o, ln_gain[None], ln_bias[None], w_dense, b_dense[None], w_out[None])

    teacher_all = remote_call(
        functools.partial(share_kernel, n_pb, n_pa),
        2,
        in_specs=[vmem],
        out_specs=vmem,
        out_shape=jax.ShapeDtypeStruct((nq, passages, nq), f32),
        scratch_shapes=[
            pltpu.SemaphoreType.DMA((nq,)),
            pltpu.SemaphoreType.DMA((nq,)),
            pltpu.SemaphoreType.DMA((1,)),
        ],
    )(teacher).reshape(total, nq)
    scores, loss, grad_query, grad_passage = call(
        loss_kernel,
        in_specs=[vmem] * 6 + [smem],
        out_shape=(
            jax.ShapeDtypeStruct((1, slots), f32),
            jax.ShapeDtypeStruct((1, 1), f32),
            jax.ShapeDtypeStruct((1, width), f32),
            jax.ShapeDtypeStruct((passages, width), f32),
        ),
        scratch_shapes=[pltpu.VMEM((total, nq), f32), pltpu.VMEM((nq, total), f32)],
    )(teacher_all, student, count, own_id, sp, sq, device)
    return scores, loss.reshape(1), grad_query, grad_passage


def solution(mesh):
    placed = (
        P(("pb", "pa"), None, None, None),
        P(("pb", "pa"), None),
        P("pb", None, None),
        P("pb", None, None),
        P("pb"),
        P(("pa", "pb"), None, None, None),
        P(("pa", "pb"), None),
        P(("pa", "pb"), None),
        P(),
        P(),
        P(),
        P(),
        P(),
        P(),
    )
    return jax.shard_map(
        functools.partial(local, mesh.shape["pb"], mesh.shape["pa"]),
        mesh=mesh,
        in_specs=placed,
        out_specs=(P(("pb", "pa"), None), P(("pb", "pa")), P(("pb", "pa"), None), P(("pa", "pb"), None)),
        check_vma=False,
    )
```

time: 231 us -> 95.5 us (0.41)
  waiting for transfers between devices: 78.7 us -> 0 us
  blocking collectives: 72.4 us -> 0 us
  Pallas kernels: 50.2 us -> 86.9 us
  between operations: 14.8 us -> 1.34 us
  local copies, waits for them, and re-layouts: 7.59 us -> 3.36 us
    all_gather x2 -> x0, waiting for transfers between devices: 78 us -> none  [the longest x1 50.1 us: local(): got = lax.all_gather(first, axes, axis=0, tiled=True)]
    all_gather x1 -> x0, blocking collectives: 72.4 us -> none  [local(): teacher_all = lax.all_gather(teacher, axes, axis=0, tiled=True)]
    pallas_call x4 -> x6, Pallas kernels: 50.2 us -> 86.9 us  [the longest x1 43.9 us: local(): remote_call(functools.partial(gather_kernel, n_pb, n_pa), 1, in_specs=[an...]
  transfers between devices with their start and end apart: 2 -> 0, of which waited for: 2 -> 0; matrix products, arithmetic and copies ran while one was open for 1% -> 0% of each run, Pallas kernels for 17% -> 0%
where the time goes in v2:
time: 95.5 us; the launch traced here: 95 us
  Pallas kernels  86.9 us (91%)
  other arithmetic  3.46 us (4%)
  local copies, waits for them, and re-layouts  3.36 us (4%)
  between operations  1.34 us (1%)
    pallas_call x1, Pallas kernels, local(): remote_call(functools.partial(gather_kernel, n_pb, n_pa), 1, in_specs=[an...  43.9 us
    pallas_call x1, Pallas kernels, local(): call(functools.partial(cross_kernel, chunk), grid_spec=pltpu.PrefetchScal...  17.7 us
    pallas_call x1, Pallas kernels, local(): remote_call(functools.partial(share_kernel, n_pb, n_pa), 2, in_specs=[vme...  12.4 us
    pallas_call x1, Pallas kernels, local(): call(functools.partial(head_kernel, step), grid_spec=pltpu.PrefetchScalar...  7.29 us
    pallas_call x1, Pallas kernels, local(): call(functools.partial(list_kernel, n_pa), grid=(1,), in_specs=[smem, pl....  3.23 us
    pallas_call x1, Pallas kernels, local(): call(loss_kernel, in_specs=[vmem] * 6 + [smem], out_shape=(jax.ShapeDtype...  2.37 us

profile of v2, /device:TPU:0, one launch (start us, length us, event | category | flops | bytes accessed | tf_op | source)
XLA Modules:
  0.0 95.0 jit_solution(3827407109225721528)
XLA Ops:
  0.6 0.0 copy-start
  0.7 1.2 %dynamic_slice.11 = s32[1]{0:T(128)} dynamic-slice(s32[4]{0:T(128)} %param.18, s32[]{:T(128)S(6)} %select_n.37), dynamic_slice_sizes={1} | dynamic-slice | bytes 12 | tf_op jit(solution)/shard_map/dynamic_slice | solution.py:434
  2.6 0.0 copy-done
  2.6 0.2 dynamic-slice_reduce_fusion
  2.8 0.1 add.64
  2.8 0.1 add.65
  2.9 0.1 pad.10.clone
  3.0 0.7 fusion.6
  3.7 0.1 reshape_squeeze.7
  3.8 0.1 fusion.4
  3.9 0.1 squeeze.12
  3.9 1.2 %compare_select_fusion.slot_ref = s32[1,64]{1,0:T(1,128)} fusion(s32[1,64]{1,0:T(1,128)S(1)} %add.65, s32[1,64]{1,0:T(1,128)S(1)} %squeeze.12, s32[]{:T(128)} %bitcast.9), kind=kLoop, calls=%fused_computation.12 | loop fusion | flops 1600 | bytes 772 | tf_op jit(solution)/shard_map/jit(_where)/select_n | solution.py:437
  5.2 0.8 maximum_bitcast_fusion
  6.0 1.5 %slice_bitcast_fusion = (bf16[1,32,1024]{2,1,0:T(8,128)(2,1)}, bf16[1,32,1024]{2,1,0:T(8,128)(2,1)S(1)}) fusion(bf16[1,2,32,1024]{3,2,1,0:T(8,128)(2,1)} %param.14), kind=kLoop, calls=%fused_computation.1 | loop fusion | bytes 262144 | tf_op jit(solution)/shard_map/squeeze | solution.py:460
  7.5 0.6 pad_maximum_fusion.first_ref
  8.1 43.9 %shard_map.165 = (bf16[32,48,1024]{2,1,0:T(8,128)(2,1)}, bf16[32,32,1024]{2,1,0:T(8,128)(2,1)}, bf16[256,1024]{1,0:T(8,128)(2,1)}, f32[8,2,256]{2,1,0:T(2,128)}) custom-call(bf16[1,48,1024]{2,1,0:T(8,128)(2,1)} %pad_maximum_fusion.first_ref, bf16[1,32,1024]{2,1,0:T(8,128)(2,1)} %get-tuple-element.36.value_ref, bf16[8,3,32,1024]{3,2,1,0:T(8,128)(2,1)} %q_ref.1), custom_call_target="tpu_custom_call" | custom-call | tf_op jit(solution)/shard_map/pallas_call | solution.py:444
  52.1 3.2 %shard_map.166 = (bf16[256,1024]{1,0:T(8,128)(2,1)}, bf16[32,1024]{1,0:T(8,128)(2,1)}, f32[256,32]{1,0:T(8,128)}, f32[256,32]{1,0:T(8,128)}, s32[2,32]{1,0:T(2,128)}) custom-call(s32[1]{0:T(128)} %bitcast.index_ref, bf16[32,48,1024]{2,1,0:T(8,128)(2,1)} %get-tuple-element.19.extra_ref.k_ref), custom_call_target="tpu_custom_call" | custom-call | tf_op jit(solution)/shard_map/pallas_call | solution.py:463
  55.3 17.7 %shard_map.167 = (bf16[8,16,1024]{2,1,0:T(8,128)(2,1)}, f32[256,1024]{1,0:T(8,128)}) custom-call(s32[2,32]{1,0:T(2,128)} %get-tuple-element.20.order_ref, bf16[32,48,1024]{2,1,0:T(8,128)(2,1)} %get-tuple-element.19.extra_ref.k_ref, bf16[8,3,32,1024]{3,2,1,0:T(8,128)(2,1)} %q_ref.1, bf16[256,1024]{1,0:T(8,128)(2,1)} %get-tuple-element.22.so_ref, ...), custom_call_target="tpu_custom_call" | custom-call | tf_op jit(solution)/shard_map/pallas_call | solution.py:482
  73.0 7.3 %shard_map.168.own_ref = f32[8,32]{1,0:T(8,128)} custom-call(s32[2,32]{1,0:T(2,128)} %get-tuple-element.20.order_ref, bf16[32,32,1024]{2,1,0:T(8,128)(2,1)} %get-tuple-element.21.v_ref, bf16[8,16,1024]{2,1,0:T(8,128)(2,1)} %get-tuple-element.24.kwt_ref, f32[256,1024]{1,0:T(8,128)} %get-tuple-element.25.part_ref, bf16[8,1024]{1,0:T(8,128)(2,1)} %resid_ref.1, ...), custom_call_target="tpu_custom_call" | custom-call | tf_op jit(solution)/shard_map/pallas_call | solution.py:505
  80.3 12.4 %shard_map.169 = f32[32,8,32]{2,1,0:T(8,128)} custom-call(f32[8,32]{1,0:T(8,128)} %shard_map.168.own_ref), custom_call_target="tpu_custom_call" | custom-call | tf_op jit(solution)/shard_map/pallas_call | solution.py:528
  92.7 2.4 %shard_map.170 = (f32[1,64]{1,0:T(1,128)}, f32[1,1]{1,0:T(1,128)}, f32[1,1024]{1,0:T(1,128)}, f32[8,1024]{1,0:T(8,128)}) custom-call(f32[256,32]{1,0:T(8,128)} %bitcast.14, f32[256,32]{1,0:T(8,128)} %get-tuple-element.26.student_ref, f32[256,32]{1,0:T(8,128)} %get-tuple-element.27.count_ref, s32[1,64]{1,0:T(1,128)} %compare_select_fusion.slot_ref, ...), custom_call_target="tpu_custom_call" | custom-call | tf_op jit(solution)/shard_map/pallas_call | solution.py:540
  (3 shorter events, 0.0 us)
Async XLA Ops:
  0.6 1.9 %copy-start = (s32[4,2,1]{0,2,1:T(1,128)S(1)}, s32[4,2,1]{0,2,1:T(1,128)}, u32[]{:S(2)}) copy-start(s32[4,2,1]{0,2,1:T(1,128)} %param.16) | copy-start | bytes 100

commit v3 on v2

--- a/solution.py
+++ b/solution.py
@@ -52,7 +52,10 @@
     lse_ref[k] = jnp.concatenate(lses, axis=0)
 
 
-def gather_kernel(n_pb, n_pa, first_ref, value_ref, qkv_ref, got_ref, vals_ref, out_ref, lse_ref, send, recv, here):
+def gather_kernel(
+    n_pb, n_pa, kv_ref, qkv_ref, sp_ref, sq_ref, cand_ref, holder_ref, count_ref,
+    got_ref, vals_ref, more_ref, out_ref, lse_ref, wide, packed, send, recv, here,
+):
     me_b, me_a = lax.axis_index("pb"), lax.axis_index("pa")
     core = me_b % 2
     spot = me_b // 2
@@ -61,120 +64,173 @@
     across = ((1 - sy) * 2 + sx) * 2 + core
     corner = ((1 - sy) * 2 + 1 - sx) * 2 + core
     other = spot * 2 + 1 - core
-    bufs = (got_ref, vals_ref)
-
-    def copy(kind, piece, slot, owner_b, to_b, to_a):
-        owner_a = (me_a + n_pa - slot) % n_pa
+    bufs = (got_ref, vals_ref, more_ref)
+    pieces = range(3)
+    mesh_ids = pl.DeviceIdType.MESH
+
+    def copy(kind, piece, owner_a, owner_b, to_b, to_a, landing=None):
         ref = bufs[piece].at[owner_b * n_pa + owner_a]
+        landing = kind if landing is None else landing
         return pltpu.make_async_remote_copy(
             src_ref=ref,
             dst_ref=ref,
-            send_sem=send.at[kind * 2 + piece, slot],
-            recv_sem=recv.at[kind * 2 + piece, slot],
+            send_sem=send.at[kind * 3 + piece, owner_a],
+            recv_sem=recv.at[landing * 3 + piece, owner_a],
             device_id=(to_b, to_a),
-            device_id_type=pl.DeviceIdType.MESH,
+            device_id_type=mesh_ids,
         )
 
-    def along(piece, step):
-        ref = bufs[piece].at[me_b * n_pa + me_a]
-        return pltpu.make_async_remote_copy(
-            src_ref=ref,
-            dst_ref=ref,
-            send_sem=send.at[piece, step],
-            recv_sem=recv.at[piece, step],
-            device_id=(me_b, (me_a + step) % n_pa),
-            device_id_type=pl.DeviceIdType.MESH,
-        )
-
-    def arrived(kind, piece, slot, owner_b):
-        copy(kind, piece, slot, owner_b, other, me_a).wait_recv()
+    def up(piece, owner_a):
+        return copy(0, piece, owner_a, me_b, me_b, me_a + 1)
+
+    def down(piece, owner_a):
+        return copy(8, piece, owner_a, me_b, me_b, me_a - 1, landing=0)
+
+    def arrived(kind, piece, owner_a, owner_b):
+        copy(kind, piece, owner_a, owner_b, other, me_a).wait_recv()
 
     barrier = pltpu.get_barrier_semaphore()
     for peer in (beside, across, other):
-        pl.semaphore_signal(barrier, inc=1, device_id=(peer, me_a), device_id_type=pl.DeviceIdType.MESH)
-
-    def greet(step, carry):
-        pl.semaphore_signal(
-            barrier, inc=1, device_id=(me_b, (me_a + step) % n_pa), device_id_type=pl.DeviceIdType.MESH
-        )
-        return carry
-
-    lax.fori_loop(1, n_pa, greet, 0)
+        pl.semaphore_signal(barrier, inc=1, device_id=(peer, me_a), device_id_type=mesh_ids)
+
+    @pl.when(me_a + 1 < n_pa)
+    def _():
+        pl.semaphore_signal(barrier, inc=1, device_id=(me_b, me_a + 1), device_id_type=mesh_ids)
+
+    @pl.when(me_a > 0)
+    def _():
+        pl.semaphore_signal(barrier, inc=1, device_id=(me_b, me_a - 1), device_id_type=mesh_ids)
+
+    passages = sp_ref.shape[0]
+    width = sp_ref.shape[1]
     mine = me_b * n_pa + me_a
     own_copies = [
-        pltpu.make_async_copy(first_ref.at[0], got_ref.at[mine], here.at[0]),
-        pltpu.make_async_copy(value_ref.at[0], vals_ref.at[mine], here.at[1]),
+        pltpu.make_async_copy(kv_ref.at[0, 0], got_ref.at[mine], here.at[0]),
+        pltpu.make_async_copy(kv_ref.at[0, 1], vals_ref.at[mine], here.at[1]),
+        pltpu.make_async_copy(packed, more_ref.at[mine], here.at[2]),
     ]
-    for one in own_copies:
-        one.start()
+    own_copies[0].start()
+    own_copies[1].start()
+    wide[...] = jnp.zeros_like(wide)
+    wide[:passages] = sp_ref[...].astype(jnp.float32)
+    wide[passages : passages + 1] = sq_ref[...].astype(jnp.float32)
+    wide[passages + 1 : passages + 2] = jnp.full((1, width), count_ref[me_a].astype(jnp.float32))
+    wide[passages + 2 : passages + 2 + BLOCKS, :BLOCK] = cand_ref[me_a].astype(jnp.float32)
+    wide[passages + 2 + BLOCKS : passages + 2 + 2 * BLOCKS] = jnp.broadcast_to(
+        holder_ref[me_a].astype(jnp.float32), (BLOCKS, width)
+    )
+    packed[...] = wide[...].astype(jnp.bfloat16)
+    own_copies[2].start()
     for one in own_copies:
         one.wait()
-    pl.semaphore_wait(barrier, n_pa + 2)
-
-    def column(step, carry):
-        along(0, step).start()
-        along(1, step).start()
+
+    @pl.when((me_a > 0) & (me_a + 1 < n_pa))
+    def _():
+        pl.semaphore_wait(barrier, 5)
+
+    @pl.when((me_a == 0) | (me_a + 1 == n_pa))
+    def _():
+        pl.semaphore_wait(barrier, 4)
+
+    def column(owner, fresh):
+        if not fresh:
+            for piece in pieces:
+                arrived(0, piece, owner, me_b)
+
+        @pl.when((owner <= me_a) & (me_a + 1 < n_pa))
+        def _():
+            for piece in pieces:
+                up(piece, owner).start()
+
+        @pl.when((owner >= me_a) & (me_a > 0))
+        def _():
+            for piece in pieces:
+                down(piece, owner).start()
+
+        for piece in pieces:
+            copy(1, piece, owner, me_b, beside, me_a).start()
+            copy(2, piece, owner, me_b, across, me_a).start()
+        for piece in pieces:
+            copy(4, piece, owner, me_b, other, me_a).start()
+
+    def forward(owner):
+        for piece in pieces:
+            near, kind = (across, 2) if piece == 1 else (beside, 1)
+            arrived(kind, piece, owner, near)
+            copy(3, piece, owner, near, beside if piece == 1 else across, me_a).start()
+            copy(6 if piece == 1 else 5, piece, owner, near, other, me_a).start()
+        for piece in pieces:
+            near, kind = (beside, 1) if piece == 1 else (across, 2)
+            arrived(kind, piece, owner, near)
+            copy(5 if piece == 1 else 6, piece, owner, near, other, me_a).start()
+
+    def last(owner):
+        for piece in pieces:
+            arrived(3, piece, owner, corner)
+            copy(7, piece, owner, corner, other, me_a).start()
+
+    def both(distance, act):
+        for owner in (me_a - distance, me_a + distance):
+            @pl.when((owner >= 0) & (owner < n_pa))
+            def _(owner=owner):
+                act(owner)
+
+    def stage(distance, carry):
+        @pl.when(distance < n_pa)
+        def _():
+            both(distance, lambda owner: column(owner, False))
+
+        @pl.when(distance < 4)
+        def _():
+            for half in range(PAIRS // 4):
+                attend_pair(qkv_ref, out_ref, lse_ref, distance * (PAIRS // 4) + half)
+
+        @pl.when(distance == 1)
+        def _():
+            forward(me_a)
+
+        @pl.when((distance > 1) & (distance <= n_pa))
+        def _():
+            both(distance - 1, forward)
+
+        @pl.when(distance == 2)
+        def _():
+            last(me_a)
+
+        @pl.when(distance > 2)
+        def _():
+            both(distance - 2, last)
+
         return carry
 
-    def plane(slot, carry):
-        @pl.when(slot > 0)
-        def _():
-            arrived(0, 0, slot, me_b)
-            arrived(0, 1, slot, me_b)
-
-        for piece in range(2):
-            copy(1, piece, slot, me_b, beside, me_a).start()
-            copy(2, piece, slot, me_b, across, me_a).start()
-            copy(4, piece, slot, me_b, other, me_a).start()
-
-        @pl.when(slot < 4)
-        def _():
-            for half in range(PAIRS // 4):
-                attend_pair(qkv_ref, out_ref, lse_ref, slot * (PAIRS // 4) + half)
+    def finish(owner, carry):
+        for piece in pieces:
+            for kind, near in ((4, me_b), (5, beside), (6, across), (7, corner)):
+                arrived(kind, piece, owner, near + 1 - 2 * core)
+                copy(kind, piece, owner, near, other, me_a).wait_send()
+            copy(1, piece, owner, me_b, beside, me_a).wait_send()
+            copy(2, piece, owner, me_b, across, me_a).wait_send()
+            if piece == 1:
+                copy(3, piece, owner, across, beside, me_a).wait_send()
+            else:
+                copy(3, piece, owner, beside, across, me_a).wait_send()
+
+        @pl.when((owner <= me_a) & (me_a + 1 < n_pa))
+        def _():
+            for piece in pieces:
+                up(piece, owner).wait_send()
+
+        @pl.when((owner >= me_a) & (me_a > 0))
+        def _():
+            for piece in pieces:
+                down(piece, owner).wait_send()
 
         return carry
 
-    def forward(slot, carry):
-        arrived(1, 0, slot, beside)
-        copy(3, 0, slot, beside, across, me_a).start()
-        copy(5, 0, slot, beside, other, me_a).start()
-        arrived(2, 1, slot, across)
-        copy(3, 1, slot, across, beside, me_a).start()
-        copy(6, 1, slot, across, other, me_a).start()
-        arrived(1, 1, slot, beside)
-        copy(5, 1, slot, beside, other, me_a).start()
-        arrived(2, 0, slot, across)
-        copy(6, 0, slot, across, other, me_a).start()
-        return carry
-
-    def last(slot, carry):
-        for piece in range(2):
-            arrived(3, piece, slot, corner)
-            copy(7, piece, slot, corner, other, me_a).start()
-        return carry
-
-    def finish(slot, carry):
-        for piece in range(2):
-            for kind, owner in ((4, me_b), (5, beside), (6, across), (7, corner)):
-                far = owner + 1 - 2 * core
-                arrived(kind, piece, slot, far)
-                copy(kind, piece, slot, owner, other, me_a).wait_send()
-            copy(1, piece, slot, me_b, beside, me_a).wait_send()
-            copy(2, piece, slot, me_b, across, me_a).wait_send()
-        copy(3, 0, slot, beside, across, me_a).wait_send()
-        copy(3, 1, slot, across, beside, me_a).wait_send()
-
-        @pl.when(slot > 0)
-        def _():
-            along(0, slot).wait_send()
-            along(1, slot).wait_send()
-
-        return carry
-
-    lax.fori_loop(1, n_pa, column, 0)
-    lax.fori_loop(0, n_pa, plane, 0)
-    lax.fori_loop(0, n_pa, forward, 0)
-    lax.fori_loop(0, n_pa, last, 0)
+    column(me_a, True)
+    for half in range(PAIRS // 4):
+        attend_pair(qkv_ref, out_ref, lse_ref, half)
+    lax.fori_loop(1, n_pa + 2, stage, 0)
     lax.fori_loop(0, n_pa, finish, 0)
 
 
@@ -232,7 +288,7 @@
     lax.fori_loop(1, count, finish, 0)
 
 
-def list_kernel(n_pa, index_ref, extra_ref, sp_ref, sq_ref, student_ref, count_ref, order_ref, held):
+def list_kernel(n_pa, index_ref, extra_ref, sp_ref, sq_ref, student_ref, count_ref, order_ref, slot_ref, held):
     queries, _, width = extra_ref.shape
     total = sp_ref.shape[0]
     passages = total // queries
@@ -243,22 +299,28 @@
     sp_ref[...] = sp
     sq_ref[...] = sq
     student_ref[...] = student_scale * lax.dot_general(sp, sq, NT, preferred_element_type=jnp.float32)
-    ids = rest[:, 1, :LANES].T
-    slots = BLOCK * BLOCKS
+    real = rest[:, 1, :LANES].T[:1]
+    ids = [rest[:, 2 + b, :LANES].T for b in range(BLOCKS)]
+    holders = [rest[:, 2 + BLOCKS + b, :LANES].T[:1] for b in range(BLOCKS)]
+    own_rest = extra_ref[pl.ds(index_ref[0], 1)].astype(jnp.float32)[0, passages:]
+    slot = own_rest[2 : 2 + BLOCKS, :BLOCK]
+    slot_group = jnp.floor(slot / passages)
+    slot_id = (slot_group * n_pa + own_rest[2 + BLOCKS : 2 + 2 * BLOCKS, :BLOCK]) * passages + slot - slot_group * passages
+    number_of = (iota((BLOCKS, BLOCK), 0) * BLOCK + iota((BLOCKS, BLOCK), 1)).astype(jnp.float32)
+    slot_ref[...] = jnp.where(number_of < own_rest[1:2, :BLOCK], slot_id, -1.0).astype(jnp.int32)
     row = iota((total, queries), 0).astype(jnp.float32)
     number = jnp.floor(row / passages)
     part = row - number * passages
     group = jnp.floor(number / n_pa)
     holder_of = number - group * n_pa
     local_of = group * passages + part
-    real = ids[slots + BLOCKS : slots + BLOCKS + 1]
     count = jnp.zeros((total, queries), jnp.float32)
     for b in range(BLOCKS):
         tally = jnp.zeros((total, queries), jnp.float32)
-        for c in range(b * BLOCK, (b + 1) * BLOCK):
-            name = jnp.where(real > c, ids[c : c + 1], -1.0)
+        for c in range(BLOCK):
+            name = jnp.where(real > b * BLOCK + c, ids[b][c : c + 1], -1.0)
             tally = tally + (local_of == name).astype(jnp.float32)
-        count = count + jnp.where(holder_of == ids[slots + b : slots + b + 1], tally, 0.0)
+        count = count + jnp.where(holder_of == holders[b], tally, 0.0)
     count_ref[...] = count
     held[...] = count
     own = held[pl.ds(pl.multiple_of(index_ref[0] * passages, passages), passages), :]
@@ -317,7 +379,7 @@
 
     @pl.when(step * queries < order_ref[1, 0])
     def _():
-        lax.fori_loop(0, PAIRS, body, 0)
+        lax.fori_loop(0, PAIRS, body, 0, unroll=4)
 
 
 def head_kernel(queries, order_ref, v_ref, kwt_ref, part_ref, resid_ref, wo_ref, gain_ref, bias_ref, wd_ref, bd_ref, out_w_ref, teacher_ref, pooled, table):
@@ -351,7 +413,7 @@
 
     @pl.when(step * queries < order_ref[1, 0])
     def _():
-        lax.fori_loop(0, PAIRS, body, 0)
+        lax.fori_loop(0, PAIRS, body, 0, unroll=4)
         mixed = jnp.dot(pooled[...], wo_ref[...], preferred_element_type=jnp.float32)
         mixed = (mixed.reshape(queries, passages, width) + resid_ref[...].astype(jnp.float32)[None]).reshape(
             queries * passages, width
@@ -379,7 +441,6 @@
 def loss_kernel(teacher_ref, student_ref, count_ref, slot_ref, sp_ref, sq_ref, index_ref, score_ref, loss_ref, gq_ref, gp_ref, held, rows_held):
     teacher, student, count = teacher_ref[...], student_ref[...], count_ref[...]
     total, queries = teacher.shape
-    slots = slot_ref.shape[1]
     passages = gp_ref.shape[0]
     index = index_ref[0]
     live = count > 0.0
@@ -396,8 +457,9 @@
     mine = iota((1, queries), 1) == index
     loss_ref[...] = jnp.sum(jnp.where(mine, loss, 0.0), axis=1, keepdims=True)
     own_teacher = jnp.sum(jnp.where(mine, teacher, 0.0), axis=1, keepdims=True)
-    hit = iota((total, slots), 0) == slot_ref[...]
-    score_ref[...] = jnp.sum(jnp.where(hit, own_teacher, 0.0), axis=0, keepdims=True)
+    for b in range(BLOCKS):
+        hit = iota((total, BLOCK), 0) == slot_ref[b : b + 1]
+        score_ref[:, b * BLOCK : (b + 1) * BLOCK] = jnp.sum(jnp.where(hit, own_teacher, 0.0), axis=0, keepdims=True)
     grad = (prob_s - prob_t) * student_scale
     held[...] = grad
     own = held[pl.ds(pl.multiple_of(index * passages, passages), passages), :]
@@ -429,53 +491,42 @@
     blocks, slot_len = cand_local.shape[1:]
     slots = blocks * slot_len
 
-    own_cand = lax.dynamic_slice_in_dim(cand_local, column, 1, 0)[0].astype(jnp.int32)
-    own_holder = lax.dynamic_slice_in_dim(block_holder, column, 1, 0)[0]
-    own_count = lax.dynamic_slice_in_dim(counts, column, 1, 0)
-    own_id = ((own_cand // passages) * n_pa + own_holder) * passages + own_cand % passages
-    own_id = own_id.reshape(1, slots)
-    own_id = jnp.where(jnp.arange(slots, dtype=jnp.int32)[None, :] < own_count[:, None], own_id, -1)
-
-    numbers = jnp.concatenate([own_cand.reshape(-1), own_holder.reshape(-1), own_count]).astype(bf16)
-    numbers = jnp.pad(numbers, (0, width - numbers.shape[0]))[None]
-    extra = jnp.concatenate([student_passage, student_query, numbers, jnp.zeros((16 - passages - 2, width), bf16)], axis=0)
-    first = jnp.concatenate([query_kv[:, 0], extra[None]], axis=1)
     anywhere, vmem, smem = (pl.BlockSpec(memory_space=m) for m in (pl.ANY, pltpu.VMEM, pltpu.SMEM))
-    got, value, self_out, self_lse = remote_call(
+    got, value, more, self_out, self_lse = remote_call(
         functools.partial(gather_kernel, n_pb, n_pa),
         1,
-        in_specs=[anywhere, anywhere, vmem],
-        out_specs=(anywhere, anywhere, vmem, vmem),
+        in_specs=[anywhere, vmem, vmem, vmem, vmem, vmem, smem],
+        out_specs=(anywhere, anywhere, anywhere, vmem, vmem),
         out_shape=(
-            jax.ShapeDtypeStruct((nq,) + first.shape[1:], bf16),
             jax.ShapeDtypeStruct((nq, keys, width), bf16),
+            jax.ShapeDtypeStruct((nq, keys, width), bf16),
+            jax.ShapeDtypeStruct((nq, 16, width), bf16),
             jax.ShapeDtypeStruct((rows, width), bf16),
             jax.ShapeDtypeStruct((PAIRS, 2, rows), f32),
         ),
         scratch_shapes=[
-            pltpu.SemaphoreType.DMA((16, n_pa)),
-            pltpu.SemaphoreType.DMA((16, n_pa)),
-            pltpu.SemaphoreType.DMA((2,)),
+            pltpu.VMEM((16, width), f32),
+            pltpu.VMEM((16, width), bf16),
+            pltpu.SemaphoreType.DMA((27, n_pa)),
+            pltpu.SemaphoreType.DMA((24, n_pa)),
+            pltpu.SemaphoreType.DMA((3,)),
         ],
-    )(first, query_kv[:, 1], passage_qkv)
+    )(query_kv, passage_qkv, student_passage, student_query, cand_local, block_holder, counts)
 
     device = index.reshape(1).astype(jnp.int32)
-    sp, sq, student, count, order = call(
+    sp, sq, student, count, order, own_id = call(
         functools.partial(list_kernel, n_pa),
-        grid=(1,),
-        in_specs=[smem, pl.BlockSpec((nq, 16, width), lambda i: (0, keys // 16, 0))],
-        out_specs=tuple(
-            pl.BlockSpec(shape, lambda i: (0, 0)) for shape in ((total, width), (nq, width), (total, nq), (total, nq), (2, nq))
-        ),
+        in_specs=[smem, vmem],
         out_shape=(
             jax.ShapeDtypeStruct((total, width), bf16),
             jax.ShapeDtypeStruct((nq, width), bf16),
             jax.ShapeDtypeStruct((total, nq), f32),
             jax.ShapeDtypeStruct((total, nq), f32),
             jax.ShapeDtypeStruct((2, nq), jnp.int32),
+            jax.ShapeDtypeStruct((blocks, slot_len), jnp.int32),
         ),
         scratch_shapes=[pltpu.VMEM((total, nq), f32)],
-    )(device, got)
+    )(device, more)
 
     whole = lambda *shape: pl.BlockSpec(shape, lambda i, o: (0,) * len(shape))
     chunk = 8

time: 95.5 us -> 76.7 us (0.80)
  Pallas kernels: 86.9 us -> 74.4 us
  other arithmetic: 3.46 us -> 0 us
  local copies, waits for them, and re-layouts: 3.36 us -> 1.36 us
    pallas_call x1, Pallas kernels: 17.7 us -> 13 us  [local(): call(functools.partial(cross_kernel, chunk), grid_spec=pltpu.PrefetchScal...]
    pallas_call x1, Pallas kernels: 43.9 us -> 39.6 us  [local(): remote_call(functools.partial(gather_kernel, n_pb, n_pa), 1, in_specs=[an...]
    pallas_call x1, Pallas kernels: 12.4 us -> 9.76 us  [local(): remote_call(functools.partial(share_kernel, n_pb, n_pa), 2, in_specs=[vme...]
    squeeze x2 -> x0, local copies, waits for them, and re-layouts: 1.59 us -> none  [the longest x1 1.51 us: local(): query_kv[:, 1]]
    dynamic_slice x2 -> x0, local copies, waits for them, and re-layouts: 1.43 us -> none  [the longest x1 1.24 us: local(): own_count = lax.dynamic_slice_in_dim(counts, column, 1, 0)]
    unnamed x2 -> x1, local copies, waits for them, and re-layouts: 0.01 us -> 1.36 us
    select_n x1 -> x0, other arithmetic: 1.23 us -> none  [local(): jnp.where(jnp.arange(slots, dtype=jnp.int32)[None, :] < own_count[:, None...]
where the time goes in v3:
time: 76.7 us; the launch traced here: 76.4 us
  Pallas kernels  74.4 us (97%)
  local copies, waits for them, and re-layouts  1.36 us (2%)
    pallas_call x1, Pallas kernels, local(): remote_call(functools.partial(gather_kernel, n_pb, n_pa), 1, in_specs=[an...  39.6 us
    pallas_call x1, Pallas kernels, local(): call(functools.partial(cross_kernel, chunk), grid_spec=pltpu.PrefetchScal...  13 us
    pallas_call x1, Pallas kernels, local(): remote_call(functools.partial(share_kernel, n_pb, n_pa), 2, in_specs=[vme...  9.76 us
    pallas_call x1, Pallas kernels, local(): call(functools.partial(head_kernel, step), grid_spec=pltpu.PrefetchScalar...  6.36 us
    pallas_call x1, Pallas kernels, local(): call(functools.partial(list_kernel, n_pa), in_specs=[smem, vmem], out_sha...  3.29 us
    pallas_call x1, Pallas kernels, local(): call(loss_kernel, in_specs=[vmem] * 6 + [smem], out_shape=(jax.ShapeDtype...  2.37 us

profile of v3, /device:TPU:0, one launch (start us, length us, event | category | flops | bytes accessed | tf_op | source)
XLA Modules:
  0.0 76.4 jit_solution(7690273742479939616)
XLA Ops:
  0.6 1.4 %copy.18.holder_ref = s32[4,2,1]{2,1,0:T(2,128)} copy(s32[4,2,1]{0,2,1:T(1,128)} %param.16) | data formatting | bytes 64 | tf_op args[2]
  2.0 39.6 %shard_map.165 = (bf16[32,32,1024]{2,1,0:T(8,128)(2,1)}, bf16[32,32,1024]{2,1,0:T(8,128)(2,1)}, bf16[32,16,1024]{2,1,0:T(8,128)(2,1)}, bf16[256,1024]{1,0:T(8,128)(2,1)}, f32[8,2,256]{2,1,0:T(2,128)}) custom-call(bf16[1,2,32,1024]{3,2,1,0:T(8,128)(2,1)} %kv_ref.1, bf16[8,3,32,1024]{3,2,1,0:T(8,128)(2,1)} %q_ref.1, bf16[8,1024]{1,0:T(8,128)(2,1)} %sp_ref.1, ...), custom_call_target="tpu_custom_call" | custom-call | tf_op jit(solution)/shard_map/pallas_call | solution.py:495
  41.6 3.3 %shard_map.166 = (bf16[256,1024]{1,0:T(8,128)(2,1)}, bf16[32,1024]{1,0:T(8,128)(2,1)}, f32[256,32]{1,0:T(8,128)}, f32[256,32]{1,0:T(8,128)}, s32[2,32]{1,0:T(2,128)}, /*index=5*/s32[2,32]{1,0:T(2,128)}) custom-call(s32[1]{0:T(128)} %bitcast.index_ref, bf16[32,16,1024]{2,1,0:T(8,128)(2,1)} %get-tuple-element.21.extra_ref), custom_call_target="tpu_custom_call" | custom-call | tf_op jit(solution)/shard_map/pallas_call | solution.py:517
  44.9 13.0 %shard_map.167 = (bf16[8,16,1024]{2,1,0:T(8,128)(2,1)}, f32[256,1024]{1,0:T(8,128)}) custom-call(s32[2,32]{1,0:T(2,128)} %get-tuple-element.22.order_ref, bf16[32,32,1024]{2,1,0:T(8,128)(2,1)} %get-tuple-element.24.k_ref, bf16[8,3,32,1024]{3,2,1,0:T(8,128)(2,1)} %q_ref.1, bf16[256,1024]{1,0:T(8,128)(2,1)} %get-tuple-element.25.so_ref, ...), custom_call_target="tpu_custom_call" | custom-call | tf_op jit(solution)/shard_map/pallas_call | solution.py:533
  57.9 6.4 %shard_map.168.own_ref = f32[8,32]{1,0:T(8,128)} custom-call(s32[2,32]{1,0:T(2,128)} %get-tuple-element.22.order_ref, bf16[32,32,1024]{2,1,0:T(8,128)(2,1)} %get-tuple-element.23.v_ref, bf16[8,16,1024]{2,1,0:T(8,128)(2,1)} %get-tuple-element.27.kwt_ref, f32[256,1024]{1,0:T(8,128)} %get-tuple-element.28.part_ref, bf16[8,1024]{1,0:T(8,128)(2,1)} %resid_ref.1, ...), custom_call_target="tpu_custom_call" | custom-call | tf_op jit(solution)/shard_map/pallas_call | solution.py:556
  64.3 9.8 %shard_map.169 = f32[32,8,32]{2,1,0:T(8,128)} custom-call(f32[8,32]{1,0:T(8,128)} %shard_map.168.own_ref), custom_call_target="tpu_custom_call" | custom-call | tf_op jit(solution)/shard_map/pallas_call | solution.py:579
  74.0 2.4 %shard_map.170 = (f32[1,64]{1,0:T(1,128)}, f32[1,1]{1,0:T(1,128)}, f32[1,1024]{1,0:T(1,128)}, f32[8,1024]{1,0:T(8,128)}) custom-call(f32[256,32]{1,0:T(8,128)} %bitcast.7, f32[256,32]{1,0:T(8,128)} %get-tuple-element.29.student_ref, f32[256,32]{1,0:T(8,128)} %get-tuple-element.30.count_ref, s32[2,32]{1,0:T(2,128)} %get-tuple-element.31.slot_ref, ...), custom_call_target="tpu_custom_call" | custom-call | tf_op jit(solution)/shard_map/pallas_call | solution.py:591

commit v4 on v3

--- a/solution.py
+++ b/solution.py
@@ -54,7 +54,7 @@
 
 def gather_kernel(
     n_pb, n_pa, kv_ref, qkv_ref, sp_ref, sq_ref, cand_ref, holder_ref, count_ref,
-    got_ref, vals_ref, more_ref, out_ref, lse_ref, wide, packed, send, recv, here,
+    vals_ref, more_ref, kwt_ref, part_ref, got_ref, out_ref, lse_ref, wide, packed, send, recv, here,
 ):
     me_b, me_a = lax.axis_index("pb"), lax.axis_index("pa")
     core = me_b % 2
@@ -180,33 +180,49 @@
         def _():
             both(distance, lambda owner: column(owner, False))
 
+        @pl.when(distance == 1)
+        def _():
+            forward(me_a)
+
+        @pl.when((distance > 1) & (distance <= n_pa))
+        def _():
+            both(distance - 1, forward)
+
+        @pl.when(distance == 2)
+        def _():
+            last(me_a)
+
+        @pl.when((distance > 2) & (distance <= n_pa + 1))
+        def _():
+            both(distance - 2, last)
+
         @pl.when(distance < 4)
         def _():
             for half in range(PAIRS // 4):
                 attend_pair(qkv_ref, out_ref, lse_ref, distance * (PAIRS // 4) + half)
 
-        @pl.when(distance == 1)
-        def _():
-            forward(me_a)
-
-        @pl.when((distance > 1) & (distance <= n_pa))
-        def _():
-            both(distance - 1, forward)
-
-        @pl.when(distance == 2)
-        def _():
-            last(me_a)
+        def score(side, inner):
+            owner = me_a + (2 * side - 1) * (distance - 3)
+
+            @pl.when((owner >= 0) & (owner < n_pa) & ((distance > 3) | (side > 0)))
+            def _():
+                for kind, near in ((4, me_b), (5, beside), (6, across), (7, corner)):
+                    arrived(kind, 0, owner, near + 1 - 2 * core)
+                cross_group(got_ref, qkv_ref, out_ref, lse_ref, kwt_ref, part_ref, owner, n_pb, n_pa)
+
+            return inner
 
         @pl.when(distance > 2)
         def _():
-            both(distance - 2, last)
+            lax.fori_loop(0, 2, score, 0)
 
         return carry
 
     def finish(owner, carry):
         for piece in pieces:
             for kind, near in ((4, me_b), (5, beside), (6, across), (7, corner)):
-                arrived(kind, piece, owner, near + 1 - 2 * core)
+                if piece > 0:
+                    arrived(kind, piece, owner, near + 1 - 2 * core)
                 copy(kind, piece, owner, near, other, me_a).wait_send()
             copy(1, piece, owner, me_b, beside, me_a).wait_send()
             copy(2, piece, owner, me_b, across, me_a).wait_send()
@@ -230,65 +246,64 @@
     column(me_a, True)
     for half in range(PAIRS // 4):
         attend_pair(qkv_ref, out_ref, lse_ref, half)
-    lax.fori_loop(1, n_pa + 2, stage, 0)
+    lax.fori_loop(1, n_pa + 3, stage, 0)
     lax.fori_loop(0, n_pa, finish, 0)
 
 
 def share_kernel(n_pb, n_pa, own_ref, all_ref, send, recv, here):
     me_b, me_a = lax.axis_index("pb"), lax.axis_index("pa")
-    count = n_pb * n_pa
-    me = me_b * n_pa + me_a
-
-    def place(step):
-        to = (me + step) % count
-        return (to // n_pa, to % n_pa)
-
-    def copy(step):
+    mesh_ids = pl.DeviceIdType.MESH
+
+    def column(step, from_a):
         return pltpu.make_async_remote_copy(
             src_ref=own_ref,
-            dst_ref=all_ref.at[me],
+            dst_ref=all_ref.at[me_b, from_a],
             send_sem=send.at[step],
             recv_sem=recv.at[step],
-            device_id=place(step),
-            device_id_type=pl.DeviceIdType.MESH,
+            device_id=(me_b, (me_a + step) % n_pa),
+            device_id_type=mesh_ids,
         )
 
-    def came(step):
-        source = (me + count - step) % count
+    def plane(step, from_b):
         return pltpu.make_async_remote_copy(
-            src_ref=own_ref,
-            dst_ref=all_ref.at[source],
-            send_sem=send.at[step],
-            recv_sem=recv.at[step],
-            device_id=place(step),
-            device_id_type=pl.DeviceIdType.MESH,
+            src_ref=all_ref.at[from_b],
+            dst_ref=all_ref.at[from_b],
+            send_sem=send.at[n_pa + step],
+            recv_sem=recv.at[n_pa + step],
+            device_id=((me_b + step) % n_pb, me_a),
+            device_id_type=mesh_ids,
         )
 
+    def loop(first, last, act):
+        def one(step, carry):
+            act(step)
+            return carry
+
+        lax.fori_loop(first, last, one, 0)
+
     barrier = pltpu.get_barrier_semaphore()
 
-    def greet(step, carry):
-        pl.semaphore_signal(barrier, inc=1, device_id=place(step), device_id_type=pl.DeviceIdType.MESH)
-        return carry
-
-    def start(step, carry):
-        copy(step).start()
-        return carry
-
-    def finish(step, carry):
-        came(step).wait_recv()
-        copy(step).wait_send()
-        return carry
-
-    lax.fori_loop(1, count, greet, 0)
-    own_copy = pltpu.make_async_copy(own_ref, all_ref.at[me], here.at[0])
+    def greet_column(step):
+        pl.semaphore_signal(barrier, inc=1, device_id=(me_b, (me_a + step) % n_pa), device_id_type=mesh_ids)
+
+    def greet_plane(step):
+        pl.semaphore_signal(barrier, inc=1, device_id=((me_b + step) % n_pb, me_a), device_id_type=mesh_ids)
+
+    loop(1, n_pa, greet_column)
+    loop(1, n_pb, greet_plane)
+    own_copy = pltpu.make_async_copy(own_ref, all_ref.at[me_b, me_a], here.at[0])
     own_copy.start()
-    pl.semaphore_wait(barrier, count - 1)
-    lax.fori_loop(1, count, start, 0)
+    pl.semaphore_wait(barrier, n_pa + n_pb - 2)
+    loop(1, n_pa, lambda step: column(step, me_a).start())
     own_copy.wait()
-    lax.fori_loop(1, count, finish, 0)
-
-
-def list_kernel(n_pa, index_ref, extra_ref, sp_ref, sq_ref, student_ref, count_ref, order_ref, slot_ref, held):
+    loop(1, n_pa, lambda step: column(step, (me_a + n_pa - step) % n_pa).wait_recv())
+    loop(1, n_pb, lambda step: plane(step, me_b).start())
+    loop(1, n_pb, lambda step: plane(step, (me_b + n_pb - step) % n_pb).wait_recv())
+    loop(1, n_pa, lambda step: column(step, me_a).wait_send())
+    loop(1, n_pb, lambda step: plane(step, me_b).wait_send())
+
+
+def list_kernel(n_pa, index_ref, extra_ref, sp_ref, sq_ref, student_ref, count_ref, slot_ref):
     queries, _, width = extra_ref.shape
     total = sp_ref.shape[0]
     passages = total // queries
@@ -322,27 +337,14 @@
             tally = tally + (local_of == name).astype(jnp.float32)
         count = count + jnp.where(holder_of == holders[b], tally, 0.0)
     count_ref[...] = count
-    held[...] = count
-    own = held[pl.ds(pl.multiple_of(index_ref[0] * passages, passages), passages), :]
-    need = (jnp.max(own, axis=0, keepdims=True) > 0.0).astype(jnp.float32)
-    lane, col = iota((queries, queries), 0), iota((queries, queries), 1)
-    need_col = jnp.sum(jnp.where(lane == col, need, 0.0), axis=1, keepdims=True)
-    before = jnp.sum(jnp.where(lane < col, need_col, 0.0), axis=0, keepdims=True)
-    needed = jnp.sum(need, axis=1, keepdims=True)
-    spot = iota((1, queries), 1).astype(jnp.float32)
-    place = jnp.where(need > 0.0, before, needed + spot - before)
-    order = jnp.sum(jnp.where(place == lane.astype(jnp.float32), col.astype(jnp.float32), 0.0), axis=1, keepdims=True)
-    order = jnp.sum(jnp.where(lane == col, order, 0.0), axis=0, keepdims=True)
-    order_ref[...] = jnp.concatenate([order, jnp.broadcast_to(needed, (1, queries))], axis=0).astype(jnp.int32)
-
-
-def cross_kernel(queries, order_ref, k_ref, q_ref, so_ref, lse_ref, kwt_ref, part_ref):
-    step = pl.program_id(0)
+
+
+def cross_group(k_ref, q_ref, so_ref, lse_ref, kwt_ref, part_ref, owner, n_pb, n_pa):
     keys = k_ref.shape[1]
     passages, _, length, _ = q_ref.shape
     rows = passages * length
     masks = pair_masks(rows)
-    out_low = iota((queries * passages, LANES), 1) < HEAD_DIM
+    out_low = iota((n_pb * passages, LANES), 1) < HEAD_DIM
     own = (iota((passages, rows), 1) // length == iota((passages, rows), 0)).astype(jnp.float32)
     spots = [
         jnp.where(iota((rows, LANES), 1) == iota((rows, LANES), 0) // length + h * passages, 1.0 / length, 0.0).astype(
@@ -354,64 +356,62 @@
     def body(k, carry):
         lanes = pl.ds(pl.multiple_of(k * LANES, LANES), LANES)
         q = q_ref[:, 0, :, lanes].reshape(rows, LANES)
-        key = jnp.concatenate([k_ref[order_ref[0, step * queries + i], :, lanes] for i in range(queries)], axis=0)
+        key = jnp.concatenate([k_ref[i * n_pa + owner, :, lanes] for i in range(n_pb)], axis=0)
         so = so_ref[:, lanes]
         lse = lse_ref[k]
         weights, parts = None, []
         for h in range(2):
             q_head = jnp.where(masks[h], q.astype(jnp.float32) * 0.125, 0.0).astype(jnp.bfloat16)
             scores = lax.dot_general(key, q_head, NT, preferred_element_type=jnp.float32)
-            scores = scores.reshape(queries, keys, rows)
+            scores = scores.reshape(n_pb, keys, rows)
             self_lse = lse[h : h + 1]
             top = jnp.maximum(jnp.max(scores, axis=1), self_lse)
             scaled = jnp.exp(scores - top[:, None, :])
             self_term = jnp.exp(self_lse - top)
             inverse = 1.0 / (jnp.sum(scaled, axis=1) + self_term)
-            spread = (scaled * inverse[:, None, :]).reshape(queries * keys, rows).astype(jnp.bfloat16)
+            spread = (scaled * inverse[:, None, :]).reshape(n_pb * keys, rows).astype(jnp.bfloat16)
             weight = jnp.dot(spread, spots[h], preferred_element_type=jnp.float32)
             weights = weight if weights is None else weights + weight
             token = self_term * inverse * (1.0 / length)
-            token = (token[:, None, :] * own[None]).reshape(queries * passages, rows).astype(jnp.bfloat16)
+            token = (token[:, None, :] * own[None]).reshape(n_pb * passages, rows).astype(jnp.bfloat16)
             parts.append(jnp.dot(token, so, preferred_element_type=jnp.float32))
-        part_ref[:, lanes] = jnp.where(out_low, parts[0], parts[1])
-        kwt_ref[k] = weights.T[: 2 * passages].astype(jnp.bfloat16)
+        part_ref[owner, :, lanes] = jnp.where(out_low, parts[0], parts[1])
+        kwt_ref[owner, k] = weights.T[: 2 * passages].astype(jnp.bfloat16)
         return carry
 
-    @pl.when(step * queries < order_ref[1, 0])
-    def _():
-        lax.fori_loop(0, PAIRS, body, 0, unroll=4)
-
-
-def head_kernel(queries, order_ref, v_ref, kwt_ref, part_ref, resid_ref, wo_ref, gain_ref, bias_ref, wd_ref, bd_ref, out_w_ref, teacher_ref, pooled, table):
+    lax.fori_loop(0, PAIRS, body, 0, unroll=4)
+
+
+def head_kernel(queries, n_pa, v_ref, kwt_ref, part_ref, resid_ref, wo_ref, gain_ref, bias_ref, wd_ref, bd_ref, out_w_ref, teacher_ref, pooled, table):
     step = pl.program_id(0)
     _, keys, width = v_ref.shape
     passages = resid_ref.shape[0]
-    group = 8
-    cols = group * keys
+    groups, _, _, cols = kwt_ref.shape
+    group = cols // keys
     span = 2 * passages
     own = (iota((group, span, cols), 2) // keys == iota((group, span, cols), 0)).astype(jnp.float32)
     low = iota((group, passages, LANES), 2) < HEAD_DIM
 
     def body(k, carry):
         lanes = pl.ds(pl.multiple_of(k * LANES, LANES), LANES)
-        for c in range(queries // group):
-            weight = kwt_ref[k, :, c * cols : (c + 1) * cols].astype(jnp.float32)
+        for c in range(groups):
+            weight = kwt_ref[c, k].astype(jnp.float32)
             weight = (weight[None] * own).reshape(group * span, cols).astype(jnp.bfloat16)
             value = jnp.concatenate(
-                [v_ref[order_ref[0, step * queries + c * group + i], :, lanes] for i in range(group)], axis=0
+                [v_ref[i * n_pa + step * groups + c, :, lanes] for i in range(group)], axis=0
             )
             got = jnp.dot(weight, value, preferred_element_type=jnp.float32)
             got = got.reshape(group, 2, passages, LANES)
             got = jnp.where(low, got[:, 0], got[:, 1]).reshape(group * passages, LANES)
             rows = slice(c * group * passages, (c + 1) * group * passages)
-            pooled[rows, lanes] = (got + part_ref[rows, lanes]).astype(jnp.bfloat16)
+            pooled[rows, lanes] = (got + part_ref[c, :, lanes]).astype(jnp.bfloat16)
         return carry
 
     @pl.when(step == 0)
     def _():
         table[...] = jnp.zeros_like(table)
 
-    @pl.when(step * queries < order_ref[1, 0])
+    @pl.when(step >= 0)
     def _():
         lax.fori_loop(0, PAIRS, body, 0, unroll=4)
         mixed = jnp.dot(pooled[...], wo_ref[...], preferred_element_type=jnp.float32)
@@ -425,7 +425,7 @@
         hidden = jnp.tanh(jnp.dot(normed, wd_ref[...], preferred_element_type=jnp.float32) + bd_ref[...])
         score = jnp.sum((hidden * out_w_ref[...]).reshape(queries, passages, width), axis=-1)
         for i in range(queries):
-            table[pl.ds(order_ref[0, step * queries + i], 1), :] = score[i : i + 1]
+            table[pl.ds(i % group * n_pa + step * groups + i // group, 1), :] = score[i : i + 1]
 
     @pl.when(step == pl.num_programs(0) - 1)
     def _():
@@ -492,19 +492,21 @@
     slots = blocks * slot_len
 
     anywhere, vmem, smem = (pl.BlockSpec(memory_space=m) for m in (pl.ANY, pltpu.VMEM, pltpu.SMEM))
-    got, value, more, self_out, self_lse = remote_call(
+    value, more, kwt, part = remote_call(
         functools.partial(gather_kernel, n_pb, n_pa),
         1,
         in_specs=[anywhere, vmem, vmem, vmem, vmem, vmem, smem],
-        out_specs=(anywhere, anywhere, anywhere, vmem, vmem),
+        out_specs=(anywhere, anywhere, vmem, vmem),
         out_shape=(
             jax.ShapeDtypeStruct((nq, keys, width), bf16),
-            jax.ShapeDtypeStruct((nq, keys, width), bf16),
             jax.ShapeDtypeStruct((nq, 16, width), bf16),
-            jax.ShapeDtypeStruct((rows, width), bf16),
-            jax.ShapeDtypeStruct((PAIRS, 2, rows), f32),
+            jax.ShapeDtypeStruct((n_pa, PAIRS, 2 * passages, n_pb * keys), bf16),
+            jax.ShapeDtypeStruct((n_pa, n_pb * passages, width), f32),
         ),
         scratch_shapes=[
+            pltpu.VMEM((nq, keys, width), bf16),
+            pltpu.VMEM((rows, width), bf16),
+            pltpu.VMEM((PAIRS, 2, rows), f32),
             pltpu.VMEM((16, width), f32),
             pltpu.VMEM((16, width), bf16),
             pltpu.SemaphoreType.DMA((27, n_pa)),
@@ -514,7 +516,7 @@
     )(query_kv, passage_qkv, student_passage, student_query, cand_local, block_holder, counts)
 
     device = index.reshape(1).astype(jnp.int32)
-    sp, sq, student, count, order, own_id = call(
+    sp, sq, student, count, own_id = call(
         functools.partial(list_kernel, n_pa),
         in_specs=[smem, vmem],
         out_shape=(
@@ -522,69 +524,42 @@
             jax.ShapeDtypeStruct((nq, width), bf16),
             jax.ShapeDtypeStruct((total, nq), f32),
             jax.ShapeDtypeStruct((total, nq), f32),
-            jax.ShapeDtypeStruct((2, nq), jnp.int32),
             jax.ShapeDtypeStruct((blocks, slot_len), jnp.int32),
         ),
-        scratch_shapes=[pltpu.VMEM((total, nq), f32)],
     )(device, more)
 
-    whole = lambda *shape: pl.BlockSpec(shape, lambda i, o: (0,) * len(shape))
-    chunk = 8
-    kwt, part = call(
-        functools.partial(cross_kernel, chunk),
-        grid_spec=pltpu.PrefetchScalarGridSpec(
-            num_scalar_prefetch=1,
-            grid=(nq // chunk,),
-            in_specs=[
-                whole(nq, keys, width),
-                whole(passages, 1, length, width),
-                whole(rows, width),
-                whole(PAIRS, 2, rows),
-            ],
-            out_specs=(
-                pl.BlockSpec((PAIRS, 2 * passages, chunk * keys), lambda i, o: (0, 0, i)),
-                pl.BlockSpec((chunk * passages, width), lambda i, o: (i, 0)),
-            ),
-        ),
-        out_shape=(
-            jax.ShapeDtypeStruct((PAIRS, 2 * passages, nq * keys), bf16),
-            jax.ShapeDtypeStruct((total, width), f32),
-        ),
-    )(order, got, passage_qkv, self_out, self_lse)
-
-    step = 16
+    whole = lambda *shape: pl.BlockSpec(shape, lambda i: (0,) * len(shape))
+    groups = 2
+    step = groups * n_pb
     teacher = call(
-        functools.partial(head_kernel, step),
-        grid_spec=pltpu.PrefetchScalarGridSpec(
-            num_scalar_prefetch=1,
-            grid=(nq // step,),
-            in_specs=[
-                whole(nq, keys, width),
-                pl.BlockSpec((PAIRS, 2 * passages, step * keys), lambda i, o: (0, 0, i)),
-                pl.BlockSpec((step * passages, width), lambda i, o: (i, 0)),
-                whole(passages, width),
-                whole(width, width),
-                whole(1, width),
-                whole(1, width),
-                whole(width, width),
-                whole(1, width),
-                whole(1, width),
-            ],
-            out_specs=whole(passages, nq),
-            scratch_shapes=[pltpu.VMEM((step * passages, width), bf16), pltpu.VMEM((nq, passages), f32)],
-        ),
+        functools.partial(head_kernel, step, n_pa),
+        grid=(n_pa // groups,),
+        in_specs=[
+            whole(nq, keys, width),
+            pl.BlockSpec((groups, PAIRS, 2 * passages, n_pb * keys), lambda i: (i, 0, 0, 0)),
+            pl.BlockSpec((groups, n_pb * passages, width), lambda i: (i, 0, 0)),
+            whole(passages, width),
+            whole(width, width),
+            whole(1, width),
+            whole(1, width),
+            whole(width, width),
+            whole(1, width),
+            whole(1, width),
+        ],
+        out_specs=whole(passages, nq),
         out_shape=jax.ShapeDtypeStruct((passages, nq), f32),
-    )(order, value, kwt, part, passage_resid, w_o, ln_gain[None], ln_bias[None], w_dense, b_dense[None], w_out[None])
+        scratch_shapes=[pltpu.VMEM((step * passages, width), bf16), pltpu.VMEM((nq, passages), f32)],
+    )(value, kwt, part, passage_resid, w_o, ln_gain[None], ln_bias[None], w_dense, b_dense[None], w_out[None])
 
     teacher_all = remote_call(
         functools.partial(share_kernel, n_pb, n_pa),
         2,
         in_specs=[vmem],
         out_specs=vmem,
-        out_shape=jax.ShapeDtypeStruct((nq, passages, nq), f32),
+        out_shape=jax.ShapeDtypeStruct((n_pb, n_pa, passages, nq), f32),
         scratch_shapes=[
-            pltpu.SemaphoreType.DMA((nq,)),
-            pltpu.SemaphoreType.DMA((nq,)),
+            pltpu.SemaphoreType.DMA((n_pa + n_pb,)),
+            pltpu.SemaphoreType.DMA((n_pa + n_pb,)),
             pltpu.SemaphoreType.DMA((1,)),
         ],
     )(teacher).reshape(total, nq)

time: 76.7 us -> 79 us (1.030)
  Pallas kernels: 74.4 us -> 76.7 us
    pallas_call x2 -> x1, Pallas kernels: 19.4 us -> 7.46 us  [local(): call(functools.partial(head_kernel, step, n_pa), grid=(n_pa // groups,),...]
    pallas_call x1, Pallas kernels: 39.6 us -> 48.7 us  [local(): remote_call(functools.partial(gather_kernel, n_pb, n_pa), 1, in_specs=[an...]
    pallas_call x1, Pallas kernels: 9.76 us -> 15.1 us  [local(): remote_call(functools.partial(share_kernel, n_pb, n_pa), 2, in_specs=[vme...]
where the time goes in v4:
time: 79 us; the launch traced here: 78.7 us
  Pallas kernels  76.7 us (97%)
  local copies, waits for them, and re-layouts  1.36 us (2%)
    pallas_call x1, Pallas kernels, local(): remote_call(functools.partial(gather_kernel, n_pb, n_pa), 1, in_specs=[an...  48.7 us
    pallas_call x1, Pallas kernels, local(): remote_call(functools.partial(share_kernel, n_pb, n_pa), 2, in_specs=[vme...  15.1 us
    pallas_call x1, Pallas kernels, local(): call(functools.partial(head_kernel, step, n_pa), grid=(n_pa // groups,),...  7.46 us
    pallas_call x1, Pallas kernels, local(): call(functools.partial(list_kernel, n_pa), in_specs=[smem, vmem], out_sha...  3.1 us
    pallas_call x1, Pallas kernels, local(): call(loss_kernel, in_specs=[vmem] * 6 + [smem], out_shape=(jax.ShapeDtype...  2.36 us

profile of v4, /device:TPU:0, one launch (start us, length us, event | category | flops | bytes accessed | tf_op | source)
XLA Modules:
  0.0 78.7 jit_solution(12418050811396362606)
XLA Ops:
  0.6 1.4 %copy.18.holder_ref = s32[4,2,1]{2,1,0:T(2,128)} copy(s32[4,2,1]{0,2,1:T(1,128)} %param.16) | data formatting | bytes 64 | tf_op args[2]
  2.0 48.7 %shard_map.165 = (bf16[32,32,1024]{2,1,0:T(8,128)(2,1)}, bf16[32,16,1024]{2,1,0:T(8,128)(2,1)}, bf16[4,8,16,256]{3,2,1,0:T(8,128)(2,1)}, f32[4,64,1024]{2,1,0:T(8,128)}) custom-call(bf16[1,2,32,1024]{3,2,1,0:T(8,128)(2,1)} %kv_ref.1, bf16[8,3,32,1024]{3,2,1,0:T(8,128)(2,1)} %qkv_ref.1, bf16[8,1024]{1,0:T(8,128)(2,1)} %sp_ref.1, bf16[1,1024]{1,0:T(2,128)(2,1)} %sq_ref.1, ...), custom_call_target="tpu_custom_call" | custom-call | tf_op jit(solution)/shard_map/pallas_call | solution.py:495
  50.7 7.5 %shard_map.166.own_ref = f32[8,32]{1,0:T(8,128)} custom-call(bf16[32,32,1024]{2,1,0:T(8,128)(2,1)} %get-tuple-element.17.v_ref, bf16[4,8,16,256]{3,2,1,0:T(8,128)(2,1)} %get-tuple-element.18.kwt_ref, f32[4,64,1024]{2,1,0:T(8,128)} %get-tuple-element.19.part_ref, bf16[8,1024]{1,0:T(8,128)(2,1)} %resid_ref.1, bf16[1024,1024]{1,0:T(8,128)(2,1)} %wo_ref.1, ...), custom_call_target="tpu_custom_call" | custom-call | tf_op jit(solution)/shard_map/pallas_call | solution.py:534
  58.1 15.1 %shard_map.167 = f32[8,4,8,32]{3,2,1,0:T(8,128)} custom-call(f32[8,32]{1,0:T(8,128)} %shard_map.166.own_ref), custom_call_target="tpu_custom_call" | custom-call | tf_op jit(solution)/shard_map/pallas_call | solution.py:554
  73.2 3.1 %shard_map.168 = (bf16[256,1024]{1,0:T(8,128)(2,1)}, bf16[32,1024]{1,0:T(8,128)(2,1)}, f32[256,32]{1,0:T(8,128)}, f32[256,32]{1,0:T(8,128)}, s32[2,32]{1,0:T(2,128)}) custom-call(s32[1]{0:T(128)} %bitcast.5.index_ref, bf16[32,16,1024]{2,1,0:T(8,128)(2,1)} %get-tuple-element.20.extra_ref), custom_call_target="tpu_custom_call" | custom-call | tf_op jit(solution)/shard_map/pallas_call | solution.py:519
  76.3 2.4 %shard_map.169 = (f32[1,64]{1,0:T(1,128)}, f32[1,1]{1,0:T(1,128)}, f32[1,1024]{1,0:T(1,128)}, f32[8,1024]{1,0:T(8,128)}) custom-call(f32[256,32]{1,0:T(8,128)} %bitcast.7, f32[256,32]{1,0:T(8,128)} %get-tuple-element.21.student_ref, f32[256,32]{1,0:T(8,128)} %get-tuple-element.22.count_ref, s32[2,32]{1,0:T(2,128)} %get-tuple-element.23.slot_ref, ...), custom_call_target="tpu_custom_call" | custom-call | tf_op jit(solution)/shard_map/pallas_call | solution.py:566

commit v5 on v4

--- a/solution.py
+++ b/solution.py
@@ -196,15 +196,15 @@
         def _():
             both(distance - 2, last)
 
-        @pl.when(distance < 4)
-        def _():
-            for half in range(PAIRS // 4):
-                attend_pair(qkv_ref, out_ref, lse_ref, distance * (PAIRS // 4) + half)
+        @pl.when(distance < 3)
+        def _():
+            for half in range(2):
+                attend_pair(qkv_ref, out_ref, lse_ref, 2 + distance * 2 + half)
 
         def score(side, inner):
-            owner = me_a + (2 * side - 1) * (distance - 3)
-
-            @pl.when((owner >= 0) & (owner < n_pa) & ((distance > 3) | (side > 0)))
+            owner = me_a + (2 * side - 1) * (distance - 2)
+
+            @pl.when((owner >= 0) & (owner < n_pa) & ((distance > 2) | (side > 0)))
             def _():
                 for kind, near in ((4, me_b), (5, beside), (6, across), (7, corner)):
                     arrived(kind, 0, owner, near + 1 - 2 * core)
@@ -212,7 +212,7 @@
 
             return inner
 
-        @pl.when(distance > 2)
+        @pl.when(distance > 1)
         def _():
             lax.fori_loop(0, 2, score, 0)
 
@@ -244,13 +244,15 @@
         return carry
 
     column(me_a, True)
-    for half in range(PAIRS // 4):
+    for half in range(4):
         attend_pair(qkv_ref, out_ref, lse_ref, half)
-    lax.fori_loop(1, n_pa + 3, stage, 0)
+    lax.fori_loop(1, n_pa + 2, stage, 0)
     lax.fori_loop(0, n_pa, finish, 0)
 
 
-def share_kernel(n_pb, n_pa, own_ref, all_ref, send, recv, here):
+def share_kernel(
+    n_pb, n_pa, own_ref, extra_ref, all_ref, sp_ref, sq_ref, student_ref, count_ref, slot_ref, send, recv, here
+):
     me_b, me_a = lax.axis_index("pb"), lax.axis_index("pa")
     mesh_ids = pl.DeviceIdType.MESH
 
@@ -298,12 +300,13 @@
     own_copy.wait()
     loop(1, n_pa, lambda step: column(step, (me_a + n_pa - step) % n_pa).wait_recv())
     loop(1, n_pb, lambda step: plane(step, me_b).start())
+    list_slots(n_pa, me_b * n_pa + me_a, extra_ref, sp_ref, sq_ref, student_ref, count_ref, slot_ref)
     loop(1, n_pb, lambda step: plane(step, (me_b + n_pb - step) % n_pb).wait_recv())
     loop(1, n_pa, lambda step: column(step, me_a).wait_send())
     loop(1, n_pb, lambda step: plane(step, me_b).wait_send())
 
 
-def list_kernel(n_pa, index_ref, extra_ref, sp_ref, sq_ref, student_ref, count_ref, slot_ref):
+def list_slots(n_pa, index, extra_ref, sp_ref, sq_ref, student_ref, count_ref, slot_ref):
     queries, _, width = extra_ref.shape
     total = sp_ref.shape[0]
     passages = total // queries
@@ -317,7 +320,7 @@
     real = rest[:, 1, :LANES].T[:1]
     ids = [rest[:, 2 + b, :LANES].T for b in range(BLOCKS)]
     holders = [rest[:, 2 + BLOCKS + b, :LANES].T[:1] for b in range(BLOCKS)]
-    own_rest = extra_ref[pl.ds(index_ref[0], 1)].astype(jnp.float32)[0, passages:]
+    own_rest = extra_ref[pl.ds(index, 1)].astype(jnp.float32)[0, passages:]
     slot = own_rest[2 : 2 + BLOCKS, :BLOCK]
     slot_group = jnp.floor(slot / passages)
     slot_id = (slot_group * n_pa + own_rest[2 + BLOCKS : 2 + 2 * BLOCKS, :BLOCK]) * passages + slot - slot_group * passages
@@ -516,18 +519,6 @@
     )(query_kv, passage_qkv, student_passage, student_query, cand_local, block_holder, counts)
 
     device = index.reshape(1).astype(jnp.int32)
-    sp, sq, student, count, own_id = call(
-        functools.partial(list_kernel, n_pa),
-        in_specs=[smem, vmem],
-        out_shape=(
-            jax.ShapeDtypeStruct((total, width), bf16),
-            jax.ShapeDtypeStruct((nq, width), bf16),
-            jax.ShapeDtypeStruct((total, nq), f32),
-            jax.ShapeDtypeStruct((total, nq), f32),
-            jax.ShapeDtypeStruct((blocks, slot_len), jnp.int32),
-        ),
-    )(device, more)
-
     whole = lambda *shape: pl.BlockSpec(shape, lambda i: (0,) * len(shape))
     groups = 2
     step = groups * n_pb
@@ -551,18 +542,26 @@
         scratch_shapes=[pltpu.VMEM((step * passages, width), bf16), pltpu.VMEM((nq, passages), f32)],
     )(value, kwt, part, passage_resid, w_o, ln_gain[None], ln_bias[None], w_dense, b_dense[None], w_out[None])
 
-    teacher_all = remote_call(
+    teacher_all, sp, sq, student, count, own_id = remote_call(
         functools.partial(share_kernel, n_pb, n_pa),
         2,
-        in_specs=[vmem],
-        out_specs=vmem,
-        out_shape=jax.ShapeDtypeStruct((n_pb, n_pa, passages, nq), f32),
+        in_specs=[vmem] * 2,
+        out_specs=(vmem,) * 6,
+        out_shape=(
+            jax.ShapeDtypeStruct((n_pb, n_pa, passages, nq), f32),
+            jax.ShapeDtypeStruct((total, width), bf16),
+            jax.ShapeDtypeStruct((nq, width), bf16),
+            jax.ShapeDtypeStruct((total, nq), f32),
+            jax.ShapeDtypeStruct((total, nq), f32),
+            jax.ShapeDtypeStruct((blocks, slot_len), jnp.int32),
+        ),
         scratch_shapes=[
             pltpu.SemaphoreType.DMA((n_pa + n_pb,)),
             pltpu.SemaphoreType.DMA((n_pa + n_pb,)),
             pltpu.SemaphoreType.DMA((1,)),
         ],
-    )(teacher).reshape(total, nq)
+    )(teacher, more)
+    teacher_all = teacher_all.reshape(total, nq)
     scores, loss, grad_query, grad_passage = call(
         loss_kernel,
         in_specs=[vmem] * 6 + [smem],

time: 79 us -> 71.7 us (0.908)
  Pallas kernels: 76.7 us -> 69.4 us
    pallas_call x1 -> x0, Pallas kernels: 3.1 us -> none  [local(): call(functools.partial(list_kernel, n_pa), in_specs=[smem, vmem], out_sha...]
    pallas_call x1, Pallas kernels: 48.7 us -> 46.3 us  [local(): remote_call(functools.partial(gather_kernel, n_pb, n_pa), 1, in_specs=[an...]
    pallas_call x1, Pallas kernels: 15.1 us -> 13.3 us  [local(): remote_call(functools.partial(share_kernel, n_pb, n_pa), 2, in_specs=[vme...]
where the time goes in v5:
time: 71.7 us; the launch traced here: 71.4 us
  Pallas kernels  69.4 us (97%)
  local copies, waits for them, and re-layouts  1.36 us (2%)
    pallas_call x1, Pallas kernels, local(): remote_call(functools.partial(gather_kernel, n_pb, n_pa), 1, in_specs=[an...  46.3 us
    pallas_call x1, Pallas kernels, local(): remote_call(functools.partial(share_kernel, n_pb, n_pa), 2, in_specs=[vme...  13.3 us
    pallas_call x1, Pallas kernels, local(): call(functools.partial(head_kernel, step, n_pa), grid=(n_pa // groups,),...  7.47 us
    pallas_call x1, Pallas kernels, local(): call(loss_kernel, in_specs=[vmem] * 6 + [smem], out_shape=(jax.ShapeDtype...  2.37 us

profile of v5, /device:TPU:0, one launch (start us, length us, event | category | flops | bytes accessed | tf_op | source)
XLA Modules:
  0.0 71.4 jit_solution(9145134297587692984)
XLA Ops:
  0.6 1.4 %copy.18.holder_ref = s32[4,2,1]{2,1,0:T(2,128)} copy(s32[4,2,1]{0,2,1:T(1,128)} %param.16) | data formatting | bytes 64 | tf_op args[2]
  2.0 46.3 %shard_map.165 = (bf16[32,32,1024]{2,1,0:T(8,128)(2,1)}, bf16[32,16,1024]{2,1,0:T(8,128)(2,1)}, bf16[4,8,16,256]{3,2,1,0:T(8,128)(2,1)}, f32[4,64,1024]{2,1,0:T(8,128)}) custom-call(bf16[1,2,32,1024]{3,2,1,0:T(8,128)(2,1)} %kv_ref.1, bf16[8,3,32,1024]{3,2,1,0:T(8,128)(2,1)} %qkv_ref.1, bf16[8,1024]{1,0:T(8,128)(2,1)} %sp_ref.1, bf16[1,1024]{1,0:T(2,128)(2,1)} %sq_ref.1, ...), custom_call_target="tpu_custom_call" | custom-call | tf_op jit(solution)/shard_map/pallas_call | solution.py:498
  48.3 7.5 %shard_map.166.own_ref = f32[8,32]{1,0:T(8,128)} custom-call(bf16[32,32,1024]{2,1,0:T(8,128)(2,1)} %get-tuple-element.18.v_ref, bf16[4,8,16,256]{3,2,1,0:T(8,128)(2,1)} %get-tuple-element.19.kwt_ref, f32[4,64,1024]{2,1,0:T(8,128)} %get-tuple-element.20.part_ref, bf16[8,1024]{1,0:T(8,128)(2,1)} %resid_ref.1, bf16[1024,1024]{1,0:T(8,128)(2,1)} %wo_ref.1, ...), custom_call_target="tpu_custom_call" | custom-call | tf_op jit(solution)/shard_map/pallas_call | solution.py:525
  55.8 13.3 %shard_map.167 = (f32[8,4,8,32]{3,2,1,0:T(8,128)}, bf16[256,1024]{1,0:T(8,128)(2,1)}, bf16[32,1024]{1,0:T(8,128)(2,1)}, f32[256,32]{1,0:T(8,128)}, f32[256,32]{1,0:T(8,128)}, /*index=5*/s32[2,32]{1,0:T(2,128)}) custom-call(f32[8,32]{1,0:T(8,128)} %shard_map.166.own_ref, bf16[32,16,1024]{2,1,0:T(8,128)(2,1)} %get-tuple-element.21.extra_ref), custom_call_target="tpu_custom_call" | custom-call | tf_op jit(solution)/shard_map/pallas_call | solution.py:545
  69.1 2.4 %shard_map.168 = (f32[1,64]{1,0:T(1,128)}, f32[1,1]{1,0:T(1,128)}, f32[1,1024]{1,0:T(1,128)}, f32[8,1024]{1,0:T(8,128)}) custom-call(f32[256,32]{1,0:T(8,128)} %bitcast.7, f32[256,32]{1,0:T(8,128)} %get-tuple-element.23.student_ref, f32[256,32]{1,0:T(8,128)} %get-tuple-element.24.count_ref, s32[2,32]{1,0:T(2,128)} %get-tuple-element.25.slot_ref, ...), custom_call_target="tpu_custom_call" | custom-call | tf_op jit(solution)/shard_map/pallas_call | solution.py:565
